TPU v7x, 512 devices: a whole 4x8x8 slice. The times are simulated.
512 devices in a mesh: seq: 128 (over z, y, core), head: 4 (over x).
Axes of the slice: x: 4, y: 8, z: 8, core: 2. Of those that a mesh axis runs over, the one named last changes fastest.
Arguments:
- queries: bfloat16 [32768, 1024], P('seq', 'head'), may hold values from -6 to 6
- keys: bfloat16 [32768, 1024], P('seq', 'head'), may hold values from -6 to 6
- values: bfloat16 [32768, 1024], P('seq', 'head'), may hold values from -8 to 8
- grad_out: bfloat16 [32768, 1024], P('seq', 'head'), may hold values from -8 to 8
- proj_weight: bfloat16 [1024, 1024], P('head'), may hold values from -0.1875 to 0.1875
Outputs:
- projected: bfloat16 [32768, 1024], P('seq', 'head')
- query_grad: bfloat16 [32768, 1024], P('seq', 'head')
- key_grad: bfloat16 [32768, 1024], P('seq', 'head')
- value_grad: bfloat16 [32768, 1024], P('seq', 'head')
- proj_grad: float32 [1024, 1024], P('head')
All inputs are finite; a program needn't handle non-finite values.
Results may differ from a plain program's by a relative error of at most 0.018.
Values may be sent and summed in bfloat16 or wider, within the bound.
A program may use at most 64 MiB of HBM per device.

v0:
```python
import math

import jax
import jax.numpy as jnp
from jax import lax
from jax.sharding import PartitionSpec as P

HEAD_DIM = 128
BLOCK = 128
LEVELS = 4


NEG = -1e30
OFFSETS = (-3, -2, 2, 3)


def shortened(array):
    return jax.tree.map(lambda a: a.astype(jnp.bfloat16) if a.dtype == jnp.float32 else a, array)


def from_behind(block, axis, distance):
    devices = range(lax.axis_size(axis))
    route = [(i - distance, i) for i in devices if i - distance in devices]
    return lax.ppermute(block, axis, route)


def partner_2(array, axis, distance):
    return lax.ppermute(array, axis, [(i, i ^ 1 << distance) for i in range(lax.axis_size(axis))])


def halve_rows(rows):
    paired = rows.astype(jnp.float32).reshape(rows.shape[0] // 2, 2, rows.shape[1])
    return (0.5 * (paired[:, 0] + paired[:, 1])).astype(jnp.bfloat16)


def spread(gradient):
    return jnp.repeat(0.5 * gradient, 2, axis=0)


def tile_mask(first_tile, tile_count, tile_total):
    tile_ids = first_tile + jnp.arange(tile_count, dtype=jnp.int32)
    columns = []
    for offset in OFFSETS:
        target = tile_ids + offset
        in_range = (target >= 0) & (target < tile_total)
        if offset == 3:
            in_range = in_range & (tile_ids % 2 == 0)
        if offset == -3:
            in_range = in_range & (tile_ids % 2 == 1)
        columns.append(in_range)
    return jnp.repeat(jnp.stack(columns, axis=1), BLOCK // 2, axis=1)


def body(queries, keys, values, grad_out, proj_weight):
    length = queries.shape[0]
    feat_width = queries.shape[1]
    heads_here = feat_width // HEAD_DIM
    blocks_here = length // BLOCK
    half_block = BLOCK // 2
    devices = lax.axis_size("seq")
    device = lax.axis_index("seq")
    score_scale = 1.0 / math.sqrt(HEAD_DIM)
    top_bit = devices.bit_length() - 1
    base_level = blocks_here.bit_length()
    local_top = min(base_level, LEVELS)
    top_level = min(LEVELS, base_level + top_bit - 2)
    joined = jnp.concatenate([keys, values], axis=1)
    coarse = [joined]
    for degree in range(1, local_top + 1):
        coarse.append(halve_rows(coarse[-1]))
    groups = []
    level_info = []
    rim_rows = {}
    for degree in range(1, local_top + 1):
        per_device = blocks_here >> degree - 1
        level_rows = coarse[degree]
        needed = sorted(
            set(
                (
                    (first_tile + offset) // per_device
                    for first_tile in range(per_device)
                    for offset in OFFSETS
                )
            )
            - {0}
        )
        received = {}
        for distance in needed:
            if degree == 1 and abs(distance) == 1:
                edge_rows = joined[:BLOCK] if distance > 0 else joined[length - BLOCK :]
                received[distance], rim_rows[distance] = (
                    from_behind(shortened(level_rows), "seq", -distance).astype(level_rows.dtype),
                    from_behind(edge_rows, "seq", -distance),
                )
            else:
                received[distance] = jax.tree.map(
                    lambda part, own: part.astype(own.dtype),
                    from_behind(shortened(level_rows), "seq", -distance),
                    level_rows,
                )
        lowest = min(needed[0], 0)
        highest = max(needed[-1], 0)
        pieces = []
        for distance in range(lowest, highest + 1):
            if distance == 0:
                pieces.append(level_rows)
            elif distance in received:
                pieces.append(received[distance])
            else:
                pieces.append(jnp.zeros_like(level_rows))
        wide_rows = jnp.concatenate(pieces, axis=0).reshape(-1, half_block, 2 * feat_width)
        base_index = -lowest * per_device
        keyset = jnp.concatenate(
            [
                wide_rows[base_index + offset : base_index + offset + per_device]
                for offset in OFFSETS
            ],
            axis=1,
        )
        groups.append(
            (per_device, keyset, tile_mask(device * per_device, per_device, devices * per_device))
        )
        level_info.append((per_device, needed, lowest, highest))
    extended = jnp.concatenate([rim_rows[-1], joined, rim_rows[1]], axis=0).reshape(
        blocks_here + 2, BLOCK, 2 * feat_width
    )
    keyset = jnp.concatenate([extended[:-2], extended[1:-1], extended[2:]], axis=1)
    block_ids = device * blocks_here + jnp.arange(blocks_here, dtype=jnp.int32)
    left_ok = jnp.broadcast_to((block_ids >= 1)[:, None], (blocks_here, BLOCK))
    right_ok = jnp.broadcast_to(
        (block_ids <= devices * blocks_here - 2)[:, None], (blocks_here, BLOCK)
    )
    near_mask = jnp.concatenate(
        [left_ok, jnp.ones((blocks_here, BLOCK), jnp.bool_), right_ok], axis=1
    )
    groups.insert(0, (blocks_here, keyset, near_mask))
    tile_rows = coarse[local_top]
    tree_info = []
    for degree in range(base_level + 1, top_level + 1):
        pair_bit = degree - base_level - 1
        partner = jax.tree.map(
            lambda part, own: part.astype(own.dtype),
            partner_2(shortened(tile_rows), "seq", pair_bit),
            tile_rows,
        )
        upper_half = device // (1 << pair_bit) % 2 == 1
        tile_rows = halve_rows(
            jnp.where(
                upper_half,
                jnp.concatenate([partner, tile_rows], axis=0),
                jnp.concatenate([tile_rows, partner], axis=0),
            )
        )
        group_span = 1 << degree - base_level
        pieces = [from_behind(tile_rows, "seq", -offset * group_span) for offset in OFFSETS]
        groups.append(
            (
                1,
                jnp.concatenate(pieces, axis=0)[None],
                tile_mask(device // group_span, 1, devices // group_span),
            )
        )
        tree_info.append((degree, group_span))
    score_list = []
    for group_count, keyset, key_mask in groups:
        per_group = length // group_count
        query_view = queries.reshape(group_count, per_group, heads_here, HEAD_DIM)
        key_view = keyset[:, :, :feat_width].reshape(group_count, -1, heads_here, HEAD_DIM)
        raw_scores = (
            jnp.einsum("grhd,gkhd->grhk", query_view, key_view, preferred_element_type=jnp.float32)
            * score_scale
        )
        score_list.append(jnp.where(key_mask[:, None, None, :], raw_scores, NEG))
    row_peak = None
    for raw_scores in score_list:
        local_peak = raw_scores.max(axis=3).reshape(length, heads_here)
        row_peak = local_peak if row_peak is None else jnp.maximum(row_peak, local_peak)
    row_total = jnp.zeros_like(row_peak)
    exp_list = []
    for group_index, raw_scores in enumerate(score_list):
        group_count = groups[group_index][0]
        peak_view = row_peak.reshape(group_count, -1, heads_here, 1)
        lifted = jnp.exp(raw_scores - peak_view)
        exp_list.append(lifted)
        row_total = row_total + lifted.sum(axis=3).reshape(length, heads_here)
    prob_list = []
    weight_list = []
    attended32 = jnp.zeros((length, heads_here, HEAD_DIM), jnp.float32)
    for (group_count, keyset, key_mask), lifted in zip(groups, exp_list):
        total_view = row_total.reshape(group_count, -1, heads_here, 1)
        group_prob = lifted / total_view
        weights = group_prob.astype(jnp.bfloat16)
        prob_list.append(group_prob)
        weight_list.append(weights)
        value_view = keyset[:, :, feat_width:].reshape(group_count, -1, heads_here, HEAD_DIM)
        attended32 = attended32 + jnp.einsum(
            "grhk,gkhd->grhd", weights, value_view, preferred_element_type=jnp.float32
        ).reshape(length, heads_here, HEAD_DIM)
    attended = attended32.reshape(length, feat_width).astype(jnp.bfloat16)
    partial_rows = jnp.dot(attended, proj_weight, preferred_element_type=jnp.float32)
    projected = lax.psum_scatter(partial_rows, "head", scatter_dimension=1, tiled=True).astype(
        jnp.bfloat16
    )
    grad_full = lax.all_gather(grad_out, "head", axis=1, tiled=True)
    attn_grad = jnp.einsum(
        "td,wd->tw", grad_full, proj_weight, preferred_element_type=jnp.float32
    ).astype(jnp.bfloat16)
    proj_grad = lax.psum(
        jnp.einsum("tw,td->wd", attended, grad_full, preferred_element_type=jnp.float32), "seq"
    )
    grad_heads = attn_grad.reshape(length, heads_here, HEAD_DIM)
    row_delta = jnp.sum(grad_heads.astype(jnp.float32) * attended32, axis=2)
    query_acc = jnp.zeros((length, heads_here, HEAD_DIM), jnp.float32)
    group_grads = []
    for (group_count, keyset, key_mask), group_prob, weights in zip(groups, prob_list, weight_list):
        per_group = length // group_count
        query_view = queries.reshape(group_count, per_group, heads_here, HEAD_DIM)
        key_view = keyset[:, :, :feat_width].reshape(group_count, -1, heads_here, HEAD_DIM)
        value_view = keyset[:, :, feat_width:].reshape(group_count, -1, heads_here, HEAD_DIM)
        grad_view = grad_heads.reshape(group_count, per_group, heads_here, HEAD_DIM)
        delta_view = row_delta.reshape(group_count, per_group, heads_here, 1)
        prob_grad = jnp.einsum(
            "grhd,gkhd->grhk", grad_view, value_view, preferred_element_type=jnp.float32
        )
        dscore = (group_prob * (prob_grad - delta_view) * score_scale).astype(jnp.bfloat16)
        query_acc = query_acc + jnp.einsum(
            "grhk,gkhd->grhd", dscore, key_view, preferred_element_type=jnp.float32
        ).reshape(length, heads_here, HEAD_DIM)
        key_part = jnp.einsum(
            "grhk,grhd->gkhd", dscore, query_view, preferred_element_type=jnp.float32
        )
        value_part = jnp.einsum(
            "grhk,grhd->gkhd", weights, grad_view, preferred_element_type=jnp.float32
        )
        num_keys = keyset.shape[1]
        group_grads.append(
            jnp.concatenate(
                [
                    key_part.reshape(group_count, num_keys, feat_width),
                    value_part.reshape(group_count, num_keys, feat_width),
                ],
                axis=2,
            )
        )
    query_grad = query_acc.reshape(length, feat_width).astype(jnp.bfloat16)
    near_grad = group_grads[0]
    padded = jnp.zeros((blocks_here + 2, BLOCK, 2 * feat_width), jnp.float32)
    padded = padded.at[:-2].add(near_grad[:, :BLOCK])
    padded = padded.at[1:-1].add(near_grad[:, BLOCK : 2 * BLOCK])
    padded = padded.at[2:].add(near_grad[:, 2 * BLOCK :])
    padded = padded.reshape(length + 2 * BLOCK, 2 * feat_width)
    level_grads = [padded[BLOCK : BLOCK + length]]
    rim_grads = {-1: padded[:BLOCK], 1: padded[length + BLOCK :]}
    for degree_index, ((per_device, needed, lowest, highest), cand_grad) in enumerate(
        zip(level_info, group_grads[1 : 1 + local_top])
    ):
        span_all = highest - lowest + 1
        wide_grad = jnp.zeros((span_all * per_device, half_block, 2 * feat_width), jnp.float32)
        base_index = -lowest * per_device
        for slot_index, offset in enumerate(OFFSETS):
            first_tile = base_index + offset
            wide_grad = wide_grad.at[first_tile : first_tile + per_device].add(
                cand_grad[:, slot_index * half_block : (slot_index + 1) * half_block]
            )
        wide_grad = wide_grad.reshape(span_all, per_device * half_block, 2 * feat_width)
        local_grad = wide_grad[-lowest]
        for distance in needed:
            if degree_index == 0 and abs(distance) == 1:
                returned, rim_returned = from_behind(
                    (wide_grad[distance - lowest], rim_grads[distance]), "seq", distance
                )
                if distance == 1:
                    level_grads[0] = level_grads[0].at[:BLOCK].add(rim_returned)
                else:
                    level_grads[0] = level_grads[0].at[length - BLOCK :].add(rim_returned)
                local_grad = local_grad + returned
            else:
                local_grad = local_grad + from_behind(
                    wide_grad[distance - lowest].astype(jnp.bfloat16), "seq", distance
                ).astype(jnp.float32)
        level_grads.append(local_grad)
    carried = jnp.zeros((half_block, 2 * feat_width), jnp.float32)
    tree_grads = group_grads[1 + local_top : 1 + local_top + len(tree_info)]
    for (degree, group_span), cand_grad in reversed(list(zip(tree_info, tree_grads))):
        for slot_index, offset in enumerate(OFFSETS):
            carried = carried + from_behind(
                shortened(cand_grad[0, slot_index * half_block : (slot_index + 1) * half_block]),
                "seq",
                offset * group_span,
            )
        pair_bit = degree - base_level - 1
        doubled = spread(carried)
        upper_half = device // (1 << pair_bit) % 2 == 1
        own_half = jnp.where(upper_half, doubled[half_block:], doubled[:half_block])
        other_half = jnp.where(upper_half, doubled[:half_block], doubled[half_block:])
        carried = own_half + partner_2(shortened(other_half), "seq", pair_bit).astype(
            other_half.dtype
        )
    if local_top == base_level:
        level_grads[local_top] = level_grads[local_top] + carried
    for degree in range(local_top, 0, -1):
        level_grads[degree - 1] = level_grads[degree - 1] + spread(level_grads[degree])
    key_grad = level_grads[0][:, :feat_width].astype(jnp.bfloat16)
    value_grad = level_grads[0][:, feat_width:].astype(jnp.bfloat16)
    return (projected, query_grad, key_grad, value_grad, proj_grad)


def solution(mesh):
    return jax.shard_map(
        body,
        mesh=mesh,
        in_specs=(
            P("seq", "head"),
            P("seq", "head"),
            P("seq", "head"),
            P("seq", "head"),
            P("head", None),
        ),
        out_specs=(
            P("seq", "head"),
            P("seq", "head"),
            P("seq", "head"),
            P("seq", "head"),
            P("head", None),
        ),
        check_vma=False,
    )
```

profile of v0, /device:TPU:1, one launch (start us, length us, event | category | flops | bytes accessed | tf_op | source)
XLA Modules:
  0.0 409.5 jit_solution(9022186685721032229)
XLA Ops:
  11.7 8.9 %collective-permute-start.10 = (bf16[64,512]{1,0:T(8,128)(2,1)S(1)}, bf16[64,512]{1,0:T(8,128)(2,1)S(1)}, u32[]{:S(2)}, u32[]{:S(2)}) collective-permute-start(bf16[64,512]{1,0:T(8,128)(2,1)S(1)} %bitcast.482), channel_id=1, source_target_pairs={{0,4},{4,0},{8,12},{12,8},{16,20},{20,16},{24,28},{28,24},{32,36},... | collective-permute-start | bytes 196616 | tf_op jit(solution)/shard_map/ppermute | solution.py:28
  23.2 4.5 %collective-permute-start.7 = (bf16[64,512]{1,0:T(8,128)(2,1)S(1)}, bf16[64,512]{1,0:T(8,128)(2,1)S(1)}, u32[]{:S(2)}, u32[]{:S(2)}) collective-permute-start(bf16[64,512]{1,0:T(8,128)(2,1)S(1)} %bitcast.485), channel_id=1, source_target_pairs={{0,8},{4,12},{8,16},{12,20},{16,24},{20,28},{24,32},{28,36},{32,40... | collective-permute-start | bytes 196616 | tf_op jit(solution)/shard_map/ppermute | solution.py:24
  27.7 5.2 %collective-permute-start.6 = (bf16[64,512]{1,0:T(8,128)(2,1)S(1)}, bf16[64,512]{1,0:T(8,128)(2,1)S(1)}, u32[]{:S(2)}, u32[]{:S(2)}) collective-permute-start(bf16[64,512]{1,0:T(8,128)(2,1)S(1)} %bitcast.486), channel_id=1, source_target_pairs={{0,12},{4,16},{8,20},{12,24},{16,28},{20,32},{24,36},{28,40},{32,4... | collective-permute-start | bytes 196616 | tf_op jit(solution)/shard_map/ppermute | solution.py:24
  35.4 11.3 %all_gather.3 = bf16[256,1024]{1,0:T(8,128)(2,1)S(1)} all-gather(bf16[256,256]{1,0:T(8,128)(2,1)S(1)} %copy-done.40), channel_id=1, replica_groups=mesh['seq'=128,'head'=4] {'head'}, dimensions={1}, use_global_device_ids=true | all-gather | bytes 655360 | tf_op jit(solution)/shard_map/all_gather | solution.py:204
  48.8 2.4 collective-permute-start
  51.6 1.9 collective-permute-start.1
  56.2 4.0 collective-permute-start.15
  64.7 5.8 %collective-permute-start.12 = (bf16[64,512]{1,0:T(8,128)(2,1)S(1)}, bf16[64,512]{1,0:T(8,128)(2,1)S(1)}, u32[]{:S(2)}, u32[]{:S(2)}) collective-permute-start(bf16[64,512]{1,0:T(8,128)(2,1)S(1)} %bitcast.492), channel_id=1, source_target_pairs={{0,16},{4,20},{8,24},{12,28},{16,32},{20,36},{24,40},{28,44},{32,4... | collective-permute-start | bytes 196616 | tf_op jit(solution)/shard_map/ppermute | solution.py:24
  70.4 5.3 %collective-permute-start.11 = (bf16[64,512]{1,0:T(8,128)(2,1)S(1)}, bf16[64,512]{1,0:T(8,128)(2,1)S(1)}, u32[]{:S(2)}, u32[]{:S(2)}) collective-permute-start(bf16[64,512]{1,0:T(8,128)(2,1)S(1)} %bitcast.493), channel_id=1, source_target_pairs={{0,24},{4,28},{8,32},{12,36},{16,40},{20,44},{24,48},{28,52},{32,5... | collective-permute-start | bytes 196616 | tf_op jit(solution)/shard_map/ppermute | solution.py:24
  77.5 4.3 %collective-permute-start.4 = (bf16[128,512]{1,0:T(8,128)(2,1)S(1)}, bf16[128,512]{1,0:T(8,128)(2,1)S(1)}, u32[]{:S(2)}, u32[]{:S(2)}) collective-permute-start(bf16[128,512]{1,0:T(8,128)(2,1)S(1)} %bitcast.498), channel_id=1, source_target_pairs={{4,0},{8,4},{12,8},{16,12},{20,16},{24,20},{28,24},{32,28},{36,32}... | collective-permute-start | bytes 393224 | tf_op jit(solution)/shard_map/ppermute | solution.py:24
  81.9 4.3 %collective-permute-start.3 = (bf16[128,512]{1,0:T(8,128)(2,1)S(1)}, bf16[128,512]{1,0:T(8,128)(2,1)S(1)}, u32[]{:S(2)}, u32[]{:S(2)}) collective-permute-start(bf16[128,512]{1,0:T(8,128)(2,1)S(1)} %bitcast.499), channel_id=1, source_target_pairs={{0,4},{4,8},{8,12},{12,16},{16,20},{20,24},{24,28},{28,32},{32,36}... | collective-permute-start | bytes 393224 | tf_op jit(solution)/shard_map/ppermute | solution.py:24
  86.2 2.3 collective-permute-start.2
  92.2 8.5 %collective-permute-start.17 = (bf16[64,512]{1,0:T(8,128)(2,1)}, bf16[64,512]{1,0:T(8,128)(2,1)}, u32[]{:S(2)}, u32[]{:S(2)}) collective-permute-start(bf16[64,512]{1,0:T(8,128)(2,1)} %bitcast.431), channel_id=1, source_target_pairs={{0,32},{4,36},{8,40},{12,44},{16,48},{20,52},{24,56},{28,60},{32,6... | collective-permute-start | bytes 196616 | tf_op jit(solution)/shard_map/ppermute | solution.py:24
  101.1 9.3 %collective-permute-start.16 = (bf16[64,512]{1,0:T(8,128)(2,1)}, bf16[64,512]{1,0:T(8,128)(2,1)}, u32[]{:S(2)}, u32[]{:S(2)}) collective-permute-start(bf16[64,512]{1,0:T(8,128)(2,1)} %bitcast.431), channel_id=1, source_target_pairs={{0,48},{4,52},{8,56},{12,60},{16,64},{20,68},{24,72},{28,76},{32,8... | collective-permute-start | bytes 196616 | tf_op jit(solution)/shard_map/ppermute | solution.py:24
  115.4 1.9 copy.142
  128.0 2.0 fusion.85
  132.6 2.3 fusion.73
  166.5 2.4 collective-permute-start.38
  169.8 6.8 %collective-permute-start.33 = (bf16[64,512]{1,0:T(8,128)(2,1)}, bf16[64,512]{1,0:T(8,128)(2,1)}, u32[]{:S(2)}, u32[]{:S(2)}) collective-permute-start(bf16[64,512]{1,0:T(8,128)(2,1)} %get-tuple-element.182), channel_id=1, source_target_pairs={{0,48},{4,52},{8,56},{12,60},{16,64},{20,68},{24,72},{28,76},{32,8... | collective-permute-start | bytes 196616 | tf_op jit(solution)/shard_map/ppermute | solution.py:24
  176.7 6.1 %collective-permute-start.32 = (bf16[64,512]{1,0:T(8,128)(2,1)}, bf16[64,512]{1,0:T(8,128)(2,1)}, u32[]{:S(2)}, u32[]{:S(2)}) collective-permute-start(bf16[64,512]{1,0:T(8,128)(2,1)} %get-tuple-element.183), channel_id=1, source_target_pairs={{0,32},{4,36},{8,40},{12,44},{16,48},{20,52},{24,56},{28,60},{32,6... | collective-permute-start | bytes 196616 | tf_op jit(solution)/shard_map/ppermute | solution.py:24
  202.6 4.3 %collective-permute-start.34 = (bf16[64,512]{1,0:T(8,128)(2,1)S(1)}, bf16[64,512]{1,0:T(8,128)(2,1)S(1)}, u32[]{:S(2)}, u32[]{:S(2)}) collective-permute-start(bf16[64,512]{1,0:T(8,128)(2,1)S(1)} %convert_element_type.267), channel_id=1, source_target_pairs={{0,8},{4,12},{8,0},{12,4},{16,24},{20,28},{24,16},{28,20},{32,40},... | collective-permute-start | bytes 196616 | tf_op jit(solution)/shard_map/ppermute | solution.py:28
  207.1 3.1 collective-permute-start.20
  210.2 9.6 %collective-permute-start.29 = (bf16[64,512]{1,0:T(8,128)(2,1)S(1)}, bf16[64,512]{1,0:T(8,128)(2,1)S(1)}, u32[]{:S(2)}, u32[]{:S(2)}) collective-permute-start(bf16[64,512]{1,0:T(8,128)(2,1)S(1)} %copy-done.51), channel_id=1, source_target_pairs={{0,12},{4,16},{8,20},{12,24},{16,28},{20,32},{24,36},{28,40},{32,4... | collective-permute-start | bytes 196616 | tf_op jit(solution)/shard_map/ppermute | solution.py:24
  219.9 2.9 collective-permute-start.28
  226.5 2.7 collective-permute-start.39
  229.3 6.0 %collective-permute-start.21 = (f32[128,512]{1,0:T(8,128)S(1)}, f32[128,512]{1,0:T(8,128)S(1)}, u32[]{:S(2)}, u32[]{:S(2)}) collective-permute-start(f32[128,512]{1,0:T(8,128)S(1)} %copy-done.36), channel_id=1, source_target_pairs={{0,4},{4,8},{8,12},{12,16},{16,20},{20,24},{24,28},{28,32},{32,36}... | collective-permute-start | bytes 786440 | tf_op jit(solution)/shard_map/ppermute | solution.py:24
  235.4 1.9 collective-permute-start.24
  237.4 3.1 collective-permute-start.23
  240.5 2.7 collective-permute-start.25
  246.6 5.0 %collective-permute-done.22 = bf16[128,512]{1,0:T(8,128)(2,1)S(1)} collective-permute-done((bf16[128,512]{1,0:T(8,128)(2,1)}, bf16[128,512]{1,0:T(8,128)(2,1)S(1)}, u32[]{:S(2)}, u32[]{:S(2)}) %collective-permute-start.22) | collective-permute-done | bytes 131104 | tf_op jit(solution)/shard_map/ppermute | solution.py:24
  255.8 144.0 %all-reduce.4.cloned.1.call-done = f32[256,1024]{1,0:T(8,128)} async-done(((f32[256,1024]{1,0:T(8,128)}), f32[256,1024]{1,0:T(8,128)}) %all-reduce.4.cloned.1.call-update) | async-done | bytes 1048592 | tf_op jit(solution)/shard_map/psum | solution.py:208
  399.7 2.3 copy.293
  (348 shorter events, 104.7 us)
Async XLA Ops:
  8.0 246.1 %reduce-scatter.2.cloned.1.call-start = ((), (), s32[]{:S(2)}) async-start(), calls=%async_computation.1 | async-start | bytes 1310720 | tf_op jit(solution)/shard_map/reduce_scatter | solution.py:201
  11.7 37.1 %collective-permute-start.10 = (bf16[64,512]{1,0:T(8,128)(2,1)S(1)}, bf16[64,512]{1,0:T(8,128)(2,1)S(1)}, u32[]{:S(2)}, u32[]{:S(2)}) collective-permute-start(bf16[64,512]{1,0:T(8,128)(2,1)S(1)} %bitcast.482), channel_id=1, source_target_pairs={{0,4},{4,0},{8,12},{12,8},{16,20},{20,16},{24,28},{28,24},{32,36},... | collective-permute-start | bytes 196616 | tf_op jit(solution)/shard_map/ppermute | solution.py:28
  20.6 31.0 %collective-permute-start.9 = (bf16[64,512]{1,0:T(8,128)(2,1)S(1)}, bf16[64,512]{1,0:T(8,128)(2,1)S(1)}, u32[]{:S(2)}, u32[]{:S(2)}) collective-permute-start(bf16[64,512]{1,0:T(8,128)(2,1)S(1)} %bitcast.483), channel_id=1, source_target_pairs={{12,0},{16,4},{20,8},{24,12},{28,16},{32,20},{36,24},{40,28},{44,3... | collective-permute-start | bytes 196616 | tf_op jit(solution)/shard_map/ppermute | solution.py:24
  21.9 31.7 %collective-permute-start.8 = (bf16[64,512]{1,0:T(8,128)(2,1)S(1)}, bf16[64,512]{1,0:T(8,128)(2,1)S(1)}, u32[]{:S(2)}, u32[]{:S(2)}) collective-permute-start(bf16[64,512]{1,0:T(8,128)(2,1)S(1)} %bitcast.484), channel_id=1, source_target_pairs={{8,0},{12,4},{16,8},{20,12},{24,16},{28,20},{32,24},{36,28},{40,32... | collective-permute-start | bytes 196616 | tf_op jit(solution)/shard_map/ppermute | solution.py:24
  23.2 31.7 %collective-permute-start.7 = (bf16[64,512]{1,0:T(8,128)(2,1)S(1)}, bf16[64,512]{1,0:T(8,128)(2,1)S(1)}, u32[]{:S(2)}, u32[]{:S(2)}) collective-permute-start(bf16[64,512]{1,0:T(8,128)(2,1)S(1)} %bitcast.485), channel_id=1, source_target_pairs={{0,8},{4,12},{8,16},{12,20},{16,24},{20,28},{24,32},{28,36},{32,40... | collective-permute-start | bytes 196616 | tf_op jit(solution)/shard_map/ppermute | solution.py:24
  27.7 28.5 %collective-permute-start.6 = (bf16[64,512]{1,0:T(8,128)(2,1)S(1)}, bf16[64,512]{1,0:T(8,128)(2,1)S(1)}, u32[]{:S(2)}, u32[]{:S(2)}) collective-permute-start(bf16[64,512]{1,0:T(8,128)(2,1)S(1)} %bitcast.486), channel_id=1, source_target_pairs={{0,12},{4,16},{8,20},{12,24},{16,28},{20,32},{24,36},{28,40},{32,4... | collective-permute-start | bytes 196616 | tf_op jit(solution)/shard_map/ppermute | solution.py:24
  48.8 15.9 %collective-permute-start = (bf16[128,512]{1,0:T(8,128)(2,1)S(1)}, bf16[128,512]{1,0:T(8,128)(2,1)S(1)}, u32[]{:S(2)}, u32[]{:S(2)}) collective-permute-start(bf16[128,512]{1,0:T(8,128)(2,1)S(1)} %get-tuple-element.195), channel_id=1, source_target_pairs={{0,4},{4,8},{8,12},{12,16},{16,20},{20,24},{24,28},{28,32},{32,36}... | collective-permute-start | bytes 393224 | tf_op jit(solution)/shard_map/ppermute | solution.py:24
  51.6 18.8 %collective-permute-start.1 = (bf16[128,512]{1,0:T(8,128)(2,1)S(1)}, bf16[128,512]{1,0:T(8,128)(2,1)S(1)}, u32[]{:S(2)}, u32[]{:S(2)}) collective-permute-start(bf16[128,512]{1,0:T(8,128)(2,1)S(1)} %get-tuple-element.196), channel_id=1, source_target_pairs={{4,0},{8,4},{12,8},{16,12},{20,16},{24,20},{28,24},{32,28},{36,32}... | collective-permute-start | bytes 393224 | tf_op jit(solution)/shard_map/ppermute | solution.py:24
  53.6 37.3 %collective-permute-start.5 = (bf16[128,512]{1,0:T(8,128)(2,1)S(1)}, bf16[128,512]{1,0:T(8,128)(2,1)S(1)}, u32[]{:S(2)}, u32[]{:S(2)}) collective-permute-start(bf16[128,512]{1,0:T(8,128)(2,1)S(1)} %bitcast.497), channel_id=1, source_target_pairs={{8,0},{12,4},{16,8},{20,12},{24,16},{28,20},{32,24},{36,28},{40,32... | collective-permute-start | bytes 393224 | tf_op jit(solution)/shard_map/ppermute | solution.py:24
  54.9 22.6 %collective-permute-start.14 = (bf16[64,512]{1,0:T(8,128)(2,1)S(1)}, bf16[64,512]{1,0:T(8,128)(2,1)S(1)}, u32[]{:S(2)}, u32[]{:S(2)}) collective-permute-start(bf16[64,512]{1,0:T(8,128)(2,1)S(1)} %bitcast.488), channel_id=1, source_target_pairs={{24,0},{28,4},{32,8},{36,12},{40,16},{44,20},{48,24},{52,28},{56,3... | collective-permute-start | bytes 196616 | tf_op jit(solution)/shard_map/ppermute | solution.py:24
  63.2 18.7 %collective-permute-start.13 = (bf16[64,512]{1,0:T(8,128)(2,1)S(1)}, bf16[64,512]{1,0:T(8,128)(2,1)S(1)}, u32[]{:S(2)}, u32[]{:S(2)}) collective-permute-start(bf16[64,512]{1,0:T(8,128)(2,1)S(1)} %bitcast.490), channel_id=1, source_target_pairs={{16,0},{20,4},{24,8},{28,12},{32,16},{36,20},{40,24},{44,28},{48,3... | collective-permute-start | bytes 196616 | tf_op jit(solution)/shard_map/ppermute | solution.py:24
  64.7 21.5 %collective-permute-start.12 = (bf16[64,512]{1,0:T(8,128)(2,1)S(1)}, bf16[64,512]{1,0:T(8,128)(2,1)S(1)}, u32[]{:S(2)}, u32[]{:S(2)}) collective-permute-start(bf16[64,512]{1,0:T(8,128)(2,1)S(1)} %bitcast.492), channel_id=1, source_target_pairs={{0,16},{4,20},{8,24},{12,28},{16,32},{20,36},{24,40},{28,44},{32,4... | collective-permute-start | bytes 196616 | tf_op jit(solution)/shard_map/ppermute | solution.py:24
  70.4 18.1 %collective-permute-start.11 = (bf16[64,512]{1,0:T(8,128)(2,1)S(1)}, bf16[64,512]{1,0:T(8,128)(2,1)S(1)}, u32[]{:S(2)}, u32[]{:S(2)}) collective-permute-start(bf16[64,512]{1,0:T(8,128)(2,1)S(1)} %bitcast.493), channel_id=1, source_target_pairs={{0,24},{4,28},{8,32},{12,36},{16,40},{20,44},{24,48},{28,52},{32,5... | collective-permute-start | bytes 196616 | tf_op jit(solution)/shard_map/ppermute | solution.py:24
  81.9 19.2 %collective-permute-start.3 = (bf16[128,512]{1,0:T(8,128)(2,1)S(1)}, bf16[128,512]{1,0:T(8,128)(2,1)S(1)}, u32[]{:S(2)}, u32[]{:S(2)}) collective-permute-start(bf16[128,512]{1,0:T(8,128)(2,1)S(1)} %bitcast.499), channel_id=1, source_target_pairs={{0,4},{4,8},{8,12},{12,16},{16,20},{20,24},{24,28},{28,32},{32,36}... | collective-permute-start | bytes 393224 | tf_op jit(solution)/shard_map/ppermute | solution.py:24
  86.2 24.4 %collective-permute-start.2 = (bf16[128,512]{1,0:T(8,128)(2,1)S(1)}, bf16[128,512]{1,0:T(8,128)(2,1)S(1)}, u32[]{:S(2)}, u32[]{:S(2)}) collective-permute-start(bf16[128,512]{1,0:T(8,128)(2,1)S(1)} %bitcast.500), channel_id=1, source_target_pairs={{0,8},{4,12},{8,16},{12,20},{16,24},{20,28},{24,32},{28,36},{32,40... | collective-permute-start | bytes 393224 | tf_op jit(solution)/shard_map/ppermute | solution.py:24
  88.5 28.8 %collective-permute-start.19 = (bf16[64,512]{1,0:T(8,128)(2,1)}, bf16[64,512]{1,0:T(8,128)(2,1)}, u32[]{:S(2)}, u32[]{:S(2)}) collective-permute-start(bf16[64,512]{1,0:T(8,128)(2,1)} %bitcast.431), channel_id=1, source_target_pairs={{48,0},{52,4},{56,8},{60,12},{64,16},{68,20},{72,24},{76,28},{80,3... | collective-permute-start | bytes 196616 | tf_op jit(solution)/shard_map/ppermute | solution.py:24
  90.9 26.4 %collective-permute-start.18 = (bf16[64,512]{1,0:T(8,128)(2,1)}, bf16[64,512]{1,0:T(8,128)(2,1)}, u32[]{:S(2)}, u32[]{:S(2)}) collective-permute-start(bf16[64,512]{1,0:T(8,128)(2,1)} %bitcast.431), channel_id=1, source_target_pairs={{32,0},{36,4},{40,8},{44,12},{48,16},{52,20},{56,24},{60,28},{64,3... | collective-permute-start | bytes 196616 | tf_op jit(solution)/shard_map/ppermute | solution.py:24
  92.2 25.1 %collective-permute-start.17 = (bf16[64,512]{1,0:T(8,128)(2,1)}, bf16[64,512]{1,0:T(8,128)(2,1)}, u32[]{:S(2)}, u32[]{:S(2)}) collective-permute-start(bf16[64,512]{1,0:T(8,128)(2,1)} %bitcast.431), channel_id=1, source_target_pairs={{0,32},{4,36},{8,40},{12,44},{16,48},{20,52},{24,56},{28,60},{32,6... | collective-permute-start | bytes 196616 | tf_op jit(solution)/shard_map/ppermute | solution.py:24
  101.1 16.2 %collective-permute-start.16 = (bf16[64,512]{1,0:T(8,128)(2,1)}, bf16[64,512]{1,0:T(8,128)(2,1)}, u32[]{:S(2)}, u32[]{:S(2)}) collective-permute-start(bf16[64,512]{1,0:T(8,128)(2,1)} %bitcast.431), channel_id=1, source_target_pairs={{0,48},{4,52},{8,56},{12,60},{16,64},{20,68},{24,72},{28,76},{32,8... | collective-permute-start | bytes 196616 | tf_op jit(solution)/shard_map/ppermute | solution.py:24
  157.4 242.3 %all-reduce.4.cloned.1.call-start = ((), (), s32[]{:S(2)}) async-start(), calls=%async_computation.2 | async-start | bytes 2097152 | tf_op jit(solution)/shard_map/psum | solution.py:208
  166.5 40.5 %collective-permute-start.38 = (bf16[64,512]{1,0:T(8,128)(2,1)}, bf16[64,512]{1,0:T(8,128)(2,1)}, u32[]{:S(2)}, u32[]{:S(2)}) collective-permute-start(bf16[64,512]{1,0:T(8,128)(2,1)} %get-tuple-element.186), channel_id=1, source_target_pairs={{0,24},{4,28},{8,32},{12,36},{16,40},{20,44},{24,48},{28,52},{32,5... | collective-permute-start | bytes 196616 | tf_op jit(solution)/shard_map/ppermute | solution.py:24
  169.8 27.2 %collective-permute-start.33 = (bf16[64,512]{1,0:T(8,128)(2,1)}, bf16[64,512]{1,0:T(8,128)(2,1)}, u32[]{:S(2)}, u32[]{:S(2)}) collective-permute-start(bf16[64,512]{1,0:T(8,128)(2,1)} %get-tuple-element.182), channel_id=1, source_target_pairs={{0,48},{4,52},{8,56},{12,60},{16,64},{20,68},{24,72},{28,76},{32,8... | collective-permute-start | bytes 196616 | tf_op jit(solution)/shard_map/ppermute | solution.py:24
  176.7 22.2 %collective-permute-start.32 = (bf16[64,512]{1,0:T(8,128)(2,1)}, bf16[64,512]{1,0:T(8,128)(2,1)}, u32[]{:S(2)}, u32[]{:S(2)}) collective-permute-start(bf16[64,512]{1,0:T(8,128)(2,1)} %get-tuple-element.183), channel_id=1, source_target_pairs={{0,32},{4,36},{8,40},{12,44},{16,48},{20,52},{24,56},{28,60},{32,6... | collective-permute-start | bytes 196616 | tf_op jit(solution)/shard_map/ppermute | solution.py:24
  182.8 17.5 %collective-permute-start.31 = (bf16[64,512]{1,0:T(8,128)(2,1)}, bf16[64,512]{1,0:T(8,128)(2,1)}, u32[]{:S(2)}, u32[]{:S(2)}) collective-permute-start(bf16[64,512]{1,0:T(8,128)(2,1)} %get-tuple-element.184), channel_id=1, source_target_pairs={{32,0},{36,4},{40,8},{44,12},{48,16},{52,20},{56,24},{60,28},{64,3... | collective-permute-start | bytes 196616 | tf_op jit(solution)/shard_map/ppermute | solution.py:24
  184.0 17.5 %collective-permute-start.30 = (bf16[64,512]{1,0:T(8,128)(2,1)}, bf16[64,512]{1,0:T(8,128)(2,1)}, u32[]{:S(2)}, u32[]{:S(2)}) collective-permute-start(bf16[64,512]{1,0:T(8,128)(2,1)} %get-tuple-element.181), channel_id=1, source_target_pairs={{48,0},{52,4},{56,8},{60,12},{64,16},{68,20},{72,24},{76,28},{80,3... | collective-permute-start | bytes 196616 | tf_op jit(solution)/shard_map/ppermute | solution.py:24
  198.9 21.0 %collective-permute-start.36 = (bf16[64,512]{1,0:T(8,128)(2,1)S(1)}, bf16[64,512]{1,0:T(8,128)(2,1)S(1)}, u32[]{:S(2)}, u32[]{:S(2)}) collective-permute-start(bf16[64,512]{1,0:T(8,128)(2,1)S(1)} %copy-done.50), channel_id=1, source_target_pairs={{16,0},{20,4},{24,8},{28,12},{32,16},{36,20},{40,24},{44,28},{48,3... | collective-permute-start | bytes 196616 | tf_op jit(solution)/shard_map/ppermute | solution.py:24
  200.2 22.6 %collective-permute-start.35 = (bf16[64,512]{1,0:T(8,128)(2,1)S(1)}, bf16[64,512]{1,0:T(8,128)(2,1)S(1)}, u32[]{:S(2)}, u32[]{:S(2)}) collective-permute-start(bf16[64,512]{1,0:T(8,128)(2,1)S(1)} %copy-done.49), channel_id=1, source_target_pairs={{24,0},{28,4},{32,8},{36,12},{40,16},{44,20},{48,24},{52,28},{56,3... | collective-permute-start | bytes 196616 | tf_op jit(solution)/shard_map/ppermute | solution.py:24
  202.6 21.5 %collective-permute-start.34 = (bf16[64,512]{1,0:T(8,128)(2,1)S(1)}, bf16[64,512]{1,0:T(8,128)(2,1)S(1)}, u32[]{:S(2)}, u32[]{:S(2)}) collective-permute-start(bf16[64,512]{1,0:T(8,128)(2,1)S(1)} %convert_element_type.267), channel_id=1, source_target_pairs={{0,8},{4,12},{8,0},{12,4},{16,24},{20,28},{24,16},{28,20},{32,40},... | collective-permute-start | bytes 196616 | tf_op jit(solution)/shard_map/ppermute | solution.py:28
  207.1 37.3 %collective-permute-start.20 = (f32[128,512]{1,0:T(8,128)}, f32[128,512]{1,0:T(8,128)S(1)}, u32[]{:S(2)}, u32[]{:S(2)}) collective-permute-start(f32[128,512]{1,0:T(8,128)} %slice_bitcast_fusion.1), channel_id=1, source_target_pairs={{4,0},{8,4},{12,8},{16,12},{20,16},{24,20},{28,24},{32,28},{36,32}... | collective-permute-start | bytes 786440 | tf_op jit(solution)/shard_map/ppermute | solution.py:24
  210.2 16.2 %collective-permute-start.29 = (bf16[64,512]{1,0:T(8,128)(2,1)S(1)}, bf16[64,512]{1,0:T(8,128)(2,1)S(1)}, u32[]{:S(2)}, u32[]{:S(2)}) collective-permute-start(bf16[64,512]{1,0:T(8,128)(2,1)S(1)} %copy-done.51), channel_id=1, source_target_pairs={{0,12},{4,16},{8,20},{12,24},{16,28},{20,32},{24,36},{28,40},{32,4... | collective-permute-start | bytes 196616 | tf_op jit(solution)/shard_map/ppermute | solution.py:24
  229.3 23.3 %collective-permute-start.21 = (f32[128,512]{1,0:T(8,128)S(1)}, f32[128,512]{1,0:T(8,128)S(1)}, u32[]{:S(2)}, u32[]{:S(2)}) collective-permute-start(f32[128,512]{1,0:T(8,128)S(1)} %copy-done.36), channel_id=1, source_target_pairs={{0,4},{4,8},{8,12},{12,16},{16,20},{20,24},{24,28},{28,32},{32,36}... | collective-permute-start | bytes 786440 | tf_op jit(solution)/shard_map/ppermute | solution.py:24
  235.4 16.1 %collective-permute-start.24 = (f32[128,512]{1,0:T(8,128)}, f32[128,512]{1,0:T(8,128)}, u32[]{:S(2)}, u32[]{:S(2)}) collective-permute-start(f32[128,512]{1,0:T(8,128)} %bitcast.115), channel_id=1, source_target_pairs={{0,4},{4,8},{8,12},{12,16},{16,20},{20,24},{24,28},{28,32},{32,36}... | collective-permute-start | bytes 786440 | tf_op jit(solution)/shard_map/ppermute | solution.py:24
  (67 other events, 549.0 us)
Sparse Core Ops, SparseCore 0:
  157.6 30.6 reduce-scatter.1
Sparse Core Ops, SparseCore 1:
  195.6 204.0 all-reduce.3
where the time goes:
time: 413 us; the launch traced here: 409 us
  waiting for transfers between devices  151 us (37%)
  starting transfers between devices  138 us (33%)
  local copies, waits for them, and re-layouts  52.1 us (13%)
  matrix products  25.6 us (6%)
  between operations  17.4 us (4%)
  other arithmetic  13.1 us (3%)
  blocking collectives  11.3 us (3%)
    psum x1, waiting for transfers between devices, body(): lax.psum(jnp.einsum('tw,td->wd', attended, grad_full, preferred_element_t...  144 us
    ppermute x36, starting transfers between devices, from_behind(): return lax.ppermute(block, axis, route)  118 us
    ppermute x4, starting transfers between devices, partner_2(): lax.ppermute(array, axis, [(i, i ^ 1 << distance) for i in range(lax.axis...  19.8 us
    all_gather x1, blocking collectives, body(): grad_full = lax.all_gather(grad_out, 'head', axis=1, tiled=True)  11.3 us
    slice x8, local copies, waits for them, and re-layouts, body(): keyset[:, :, feat_width:].reshape(group_count, -1, heads_here, HEAD_DIM)  8.49 us
  transfers between devices with their start and end apart: 42, of which 4 were waited for; matrix products, arithmetic and copies ran while one was open for 11% of the time, Pallas kernels for 0%

commit v1 on v0

v1 whole, which is shorter than its diff:
```python
import functools
import math

import jax
import jax.numpy as jnp
from jax import lax
from jax.experimental import pallas as pl
from jax.experimental.pallas import tpu as pltpu
from jax.sharding import PartitionSpec as P

HEAD_DIM = 128
BLOCK = 128
HALF = BLOCK // 2
ROWS = 256
FEAT = 256
HEADS_HERE = FEAT // HEAD_DIM
NEAR = 3 * BLOCK
OWN_KEYS = NEAR + 3 * HALF
UPPER = 9 * HALF
NEG = -1e30
SCALE = 1.0 / math.sqrt(HEAD_DIM)
EXP2_SCALE = SCALE * math.log2(math.e)
MESH = pl.DeviceIdType.MESH
F32 = jnp.float32
BF16 = jnp.bfloat16


def dot(a, b):
    return lax.dot_general(a, b, (((1,), (0,)), ((), ())), preferred_element_type=F32)


def dot_nt(a, b):
    return lax.dot_general(a, b, (((1,), (1,)), ((), ())), preferred_element_type=F32)


def dot_tn(a, b):
    return lax.dot_general(a, b, (((0,), (0,)), ((), ())), preferred_element_type=F32)


def pair_average(rows):
    row = lax.broadcasted_iota(jnp.int32, (rows // 2, rows), 0)
    column = lax.broadcasted_iota(jnp.int32, (rows // 2, rows), 1)
    return jnp.where((column >= 2 * row) & (column < 2 * row + 2), 0.5, 0.0).astype(BF16)


def spread_matrix():
    parts = []
    for level in range(1, 5):
        count = ROWS >> level
        token = lax.broadcasted_iota(jnp.int32, (ROWS, count), 0)
        first = lax.broadcasted_iota(jnp.int32, (ROWS, count), 1) * (1 << level)
        inside = (token >= first) & (token < first + (1 << level))
        parts.append(jnp.where(inside, 0.5**level, 0.0).astype(BF16))
    return parts


def kernel(
    devices, heads, zs, ys,
    q_ref, k_ref, v_ref, go_ref, w_ref,
    proj_ref, dq_ref, dk_ref, dv_ref, pg_ref,
    ext, lv1, own, up, gfull, gext, g1, gu, got_near, got1, got2, got3, got4,
    part, got_part, s_own, s_up, e_near, pg32, pg16, got_half, mine, got_z, cross, got_y, final,
    row_send, row_recv, grad_send, grad_recv, x_send, x_recv, red_send, red_recv,
):
    d = lax.axis_index("seq")
    h = lax.axis_index("head")
    core = lax.rem(d, 2)
    y = lax.rem(d // 2, ys)
    z = d // (2 * ys)
    sibling = d + 1 - 2 * core

    def at(target):
        return (lax.rem(target + 2 * devices, devices), h)

    def send(src, dst, send_sem, recv_sem, target):
        copy = pltpu.make_async_remote_copy(
            src_ref=src, dst_ref=dst, send_sem=send_sem, recv_sem=recv_sem,
            device_id=target, device_id_type=MESH,
        )
        copy.start()

    def arrived(ref, sem):
        pltpu.make_async_copy(ref, ref, sem).wait()

    def far(index, total):
        parity = lax.rem(index, 2)
        wide = 3 - 6 * parity
        return [lax.rem(index + o + total, total) for o in (2, -2, wide)]

    two = [(at(t)) for t in far(d, devices)]
    chip = d // 2
    three = [[(2 * t + c, h) for c in range(2)] for t in far(chip, devices // 2)]
    quad = d // 4
    place = lax.rem(d, 4)
    four = [[(4 * t + i, h) for i in range(4)] for t in far(quad, devices // 4)]
    left, right = at(d - 1), at(d + 1)
    across = [(d, lax.rem(h + r, heads)) for r in range(1, heads)]
    z_peers = [(lax.rem(z + r, zs) * (2 * ys) + 2 * y + core, h) for r in range(1, zs)]
    y_peers = [(z * (2 * ys) + 2 * lax.rem(y + r, ys) + core, h) for r in range(1, ys)]

    barrier = pltpu.get_barrier_semaphore()
    everyone = [left, right, *two, *sum(three, []), *sum(four, []), *across, *z_peers, *y_peers]
    everyone.append((sibling, h))
    for target in everyone:
        pl.semaphore_signal(barrier, inc=1, device_id=target, device_id_type=MESH)

    own_rows = slice(BLOCK, BLOCK + ROWS)
    ext[own_rows, :FEAT] = k_ref[...]
    ext[own_rows, FEAT:] = v_ref[...]
    gfull[h] = go_ref[...]
    rows = jnp.concatenate([k_ref[...], v_ref[...]], axis=1)
    offset = 0
    for level in range(1, 5):
        rows = dot(pair_average(rows.shape[0]), rows).astype(BF16)
        own[offset : offset + rows.shape[0]] = rows
        offset += rows.shape[0]
    pl.semaphore_wait(barrier, len(everyone))

    for slot in range(3):
        dst = up.at[pl.ds(pl.multiple_of(6 * HALF + slot * HALF + place * 16, 16), 16)]
        for target in four[slot]:
            send(own.at[224:240], dst, row_send, row_recv.at[4], target)
    for slot in range(3):
        dst = up.at[pl.ds(pl.multiple_of(3 * HALF + slot * HALF + core * 32, 16), 32)]
        for target in three[slot]:
            send(own.at[192:224], dst, row_send, row_recv.at[3], target)
    for r, target in enumerate(across):
        send(go_ref, gfull.at[h], x_send, x_recv.at[0], target)
    for slot in range(3):
        send(own.at[128:192], up.at[slot * HALF : (slot + 1) * HALF], row_send, row_recv.at[2], two[slot])
    send(ext.at[BLOCK : 2 * BLOCK], ext.at[3 * BLOCK :], row_send, row_recv.at[0], left)
    send(ext.at[2 * BLOCK : 3 * BLOCK], ext.at[:BLOCK], row_send, row_recv.at[0], right)
    for tile in range(2):
        tile_rows = own.at[tile * HALF : (tile + 1) * HALF]
        send(tile_rows, lv1.at[2 * tile * HALF : (2 * tile + 1) * HALF], row_send, row_recv.at[1], left)
        send(tile_rows, lv1.at[(2 * tile + 1) * HALF : (2 * tile + 2) * HALF], row_send, row_recv.at[1], right)

    if heads > 1:
        arrived(gfull.at[0 : heads - 1], x_recv.at[0])
    grad_full = jnp.concatenate([gfull[r] for r in range(heads)], axis=1)
    grad = dot_nt(grad_full, w_ref[...]).astype(BF16)
    grad_t = dot_nt(w_ref[...], grad_full).astype(BF16)

    def bias(valid):
        return jnp.where(valid, 0.0, NEG).astype(F32)

    left_bias, right_bias = bias(d >= 1), bias(d <= devices - 2)

    def far_bias(index, total):
        wide = index + 3 - 6 * lax.rem(index, 2)
        return [bias(index >= 2), bias(index + 2 < total), bias((wide >= 0) & (wide < total))]

    up_bias = far_bias(d, devices) + far_bias(chip, devices // 2) + far_bias(quad, devices // 4)

    def head_cols(head):
        return slice(head * HEAD_DIM, (head + 1) * HEAD_DIM)

    def value_cols(head):
        return slice(FEAT + head * HEAD_DIM, FEAT + (head + 1) * HEAD_DIM)

    def block_keys(block, cols):
        near = ext[block * BLOCK : block * BLOCK + NEAR, cols]
        return jnp.concatenate([near, lv1[block * HALF : block * HALF + 3 * HALF, cols]], axis=0)

    def block_queries(block, head):
        return q_ref[block * BLOCK : (block + 1) * BLOCK, head_cols(head)]

    arrived(ext.at[: 2 * BLOCK], row_recv.at[0])
    arrived(lv1, row_recv.at[1])
    own_peak = [[None] * 2 for _ in range(HEADS_HERE)]
    for head in range(HEADS_HERE):
        for block in range(2):
            scores = dot_nt(block_keys(block, head_cols(head)), block_queries(block, head))
            if block == 0:
                pieces = [
                    scores[:BLOCK] + left_bias,
                    scores[BLOCK:NEAR],
                    scores[NEAR : NEAR + HALF] + right_bias,
                    scores[NEAR + HALF : NEAR + 2 * HALF] + left_bias,
                    scores[NEAR + 2 * HALF :] + right_bias,
                ]
            else:
                pieces = [
                    scores[: 2 * BLOCK],
                    scores[2 * BLOCK : NEAR] + right_bias,
                    scores[NEAR : NEAR + HALF] + left_bias,
                    scores[NEAR + HALF : NEAR + 2 * HALF] + right_bias,
                    scores[NEAR + 2 * HALF :] + left_bias,
                ]
            scores = jnp.concatenate(pieces, axis=0)
            s_own[head, block] = scores
            own_peak[head][block] = scores.max(axis=0, keepdims=True)
    arrived(up.at[: 3 * HALF], row_recv.at[2])
    arrived(up.at[3 * HALF : 6 * HALF], row_recv.at[3])
    arrived(up.at[6 * HALF :], row_recv.at[4])
    att_t = []
    inverse = []
    for head in range(HEADS_HERE):
        raw = dot_nt(up[:, head_cols(head)], q_ref[:, head_cols(head)])
        raw = jnp.concatenate(
            [raw[i * HALF : (i + 1) * HALF] + up_bias[i] for i in range(9)], axis=0
        )
        peak = jnp.maximum(jnp.concatenate(own_peak[head], axis=1), raw.max(axis=0, keepdims=True))
        lifted_up = jnp.exp2((raw - peak) * EXP2_SCALE)
        total = lifted_up.sum(axis=0, keepdims=True)
        own_total = []
        for block in range(2):
            block_peak = peak[:, block * BLOCK : (block + 1) * BLOCK]
            lifted = jnp.exp2((s_own[head, block] - block_peak) * EXP2_SCALE)
            s_own[head, block] = lifted
            own_total.append(lifted.sum(axis=0, keepdims=True))
        inv = 1.0 / (total + jnp.concatenate(own_total, axis=1))
        prob_up = lifted_up * inv
        s_up[head] = prob_up
        up_att = dot_tn(up[:, value_cols(head)], prob_up.astype(BF16))
        own_att = []
        for block in range(2):
            prob = s_own[head, block] * inv[:, block * BLOCK : (block + 1) * BLOCK]
            s_own[head, block] = prob
            own_att.append(dot_tn(block_keys(block, value_cols(head)), prob.astype(BF16)))
        att_t.append(up_att + jnp.concatenate(own_att, axis=1))
    att32_t = jnp.concatenate(att_t, axis=0)
    att16_t = att32_t.astype(BF16)

    for side in range(2):
        half = dot(att16_t[side * BLOCK : (side + 1) * BLOCK], grad_full)
        pg32[side] = half
        pg16[side] = half.astype(BF16)
    send(pg16.at[1 - core], got_half, red_send, red_recv.at[0], (sibling, h))

    att16 = att16_t.T
    partial = dot(att16, w_ref[...])
    for r in range(heads):
        part[r] = partial[:, r * FEAT : (r + 1) * FEAT].astype(BF16)
    for r, target in enumerate(across):
        send(part.at[target[1]], got_part.at[r], x_send, x_recv.at[1], target)

    delta = []
    dq_t = []
    for head in range(HEADS_HERE):
        g_t = grad_t[head_cols(head)]
        delta.append((g_t.astype(F32) * att_t[head]).sum(axis=0, keepdims=True))
        prob = s_up[head]
        dprob = dot(up[:, value_cols(head)], g_t)
        dscore = (prob * (dprob - delta[head]) * SCALE).astype(BF16)
        dq_t.append(dot_tn(up[:, head_cols(head)], dscore))
        gu[:, head_cols(head)] = dot(dscore, q_ref[:, head_cols(head)]).astype(BF16)
        gu[:, value_cols(head)] = dot(prob.astype(BF16), grad[:, head_cols(head)]).astype(BF16)
    for slot in range(3):
        for i, target in enumerate(four[(1, 0, 2)[slot]]):
            src = gu.at[6 * HALF + slot * HALF + i * 16 : 6 * HALF + slot * HALF + (i + 1) * 16]
            send(src, got4.at[slot * 4 + place], grad_send, grad_recv.at[4], target)
    for slot in range(3):
        for c, target in enumerate(three[(1, 0, 2)[slot]]):
            src = gu.at[3 * HALF + slot * HALF + c * 32 : 3 * HALF + slot * HALF + (c + 1) * 32]
            send(src, got3.at[slot * 2 + core], grad_send, grad_recv.at[3], target)
    for slot in range(3):
        src = gu.at[slot * HALF : (slot + 1) * HALF]
        send(src, got2.at[slot], grad_send, grad_recv.at[2], two[(1, 0, 2)[slot]])

    arrived(got_half, red_recv.at[0])
    chunk = BLOCK // zs
    for i in range(zs):
        window = slice(i * chunk, (i + 1) * chunk)
        mine[i] = (pg32[core, window] + got_half[window].astype(F32)).astype(BF16)
    for r, target in enumerate(z_peers):
        send(mine.at[lax.rem(z + r + 1, zs)], got_z.at[r], red_send, red_recv.at[1], target)

    for head in range(HEADS_HERE):
        own_dq = []
        for block in range(2):
            cols = slice(block * BLOCK, (block + 1) * BLOCK)
            prob = s_own[head, block]
            dprob = dot(block_keys(block, value_cols(head)), grad_t[head_cols(head), cols])
            dscore = (prob * (dprob - delta[head][:, cols]) * SCALE).astype(BF16)
            own_dq.append(dot_tn(block_keys(block, head_cols(head)), dscore))
            dkey = dot(dscore, block_queries(block, head))
            dval = dot(prob.astype(BF16), grad[cols, head_cols(head)])
            for grads, column in ((dkey, head_cols(head)), (dval, value_cols(head))):
                if block == 0:
                    gext[:BLOCK, column] = grads[:BLOCK].astype(BF16)
                    e_near[:, column] = grads[BLOCK:NEAR]
                    g1[: 3 * HALF, column] = grads[NEAR:]
                else:
                    e_near[:, column] = e_near[:, column] + grads[: 2 * BLOCK]
                    gext[BLOCK : 2 * BLOCK, column] = grads[2 * BLOCK : NEAR].astype(BF16)
                    g1[HALF : 3 * HALF, column] = g1[HALF : 3 * HALF, column] + grads[NEAR : NEAR + 2 * HALF]
                    g1[3 * HALF :, column] = grads[NEAR + 2 * HALF :]
        dq_t[head] = dq_t[head] + jnp.concatenate(own_dq, axis=1)
    for tile in range(2):
        gext[2 * BLOCK + tile * HALF : 2 * BLOCK + (tile + 1) * HALF] = g1[
            (2 * tile + 1) * HALF : (2 * tile + 2) * HALF
        ].astype(BF16)
        gext[3 * BLOCK + tile * HALF : 3 * BLOCK + (tile + 1) * HALF] = g1[
            2 * tile * HALF : (2 * tile + 1) * HALF
        ].astype(BF16)
    send(gext.at[:BLOCK], got_near.at[1], grad_send, grad_recv.at[0], left)
    send(gext.at[BLOCK : 2 * BLOCK], got_near.at[0], grad_send, grad_recv.at[0], right)
    send(gext.at[2 * BLOCK : 3 * BLOCK], got1.at[1], grad_send, grad_recv.at[1], left)
    send(gext.at[3 * BLOCK :], got1.at[0], grad_send, grad_recv.at[1], right)
    dq_ref[...] = jnp.concatenate(dq_t, axis=0).T.astype(BF16)

    arrived(got_z, red_recv.at[1])
    total = mine[z].astype(F32)
    for r in range(zs - 1):
        total = total + got_z[r].astype(F32)
    width = cross.shape[2]
    for i in range(ys):
        cross[i] = total[:, i * width : (i + 1) * width].astype(BF16)
    for r, target in enumerate(y_peers):
        send(cross.at[lax.rem(y + r + 1, ys)], got_y.at[r], red_send, red_recv.at[2], target)

    if heads > 1:
        arrived(got_part, x_recv.at[1])
    projected = part[h].astype(F32)
    for r in range(heads - 1):
        projected = projected + got_part[r].astype(F32)
    proj_ref[...] = projected.astype(BF16)

    arrived(got_y, red_recv.at[2])
    total = cross[y].astype(F32)
    for r in range(ys - 1):
        total = total + got_y[r].astype(F32)
    final[core, z, y] = total.astype(BF16)
    for r, target in enumerate(y_peers):
        send(final.at[core, z, y], final.at[core, z, y], red_send, red_recv.at[3], target)

    arrived(got4, grad_recv.at[4])
    arrived(got3, grad_recv.at[3])
    arrived(got2, grad_recv.at[2])
    arrived(got1, grad_recv.at[1])
    arrived(got_near, grad_recv.at[0])
    levels = spread_matrix()
    rows_grad = e_near[...] + jnp.concatenate([got_near[0], got_near[1]], axis=0).astype(F32)
    for level, got in enumerate((got1, got2, got3, got4)):
        total = got[0].astype(F32)
        for i in range(1, got.shape[0]):
            total = total + got[i].astype(F32)
        rows_grad = rows_grad + dot(levels[level], total.astype(BF16))
    dk_ref[...] = rows_grad[:, :FEAT].astype(BF16)
    dv_ref[...] = rows_grad[:, FEAT:].astype(BF16)

    arrived(got_y, red_recv.at[3])
    for r, target in enumerate(z_peers):
        send(final.at[core, z], final.at[core, z], red_send, red_recv.at[4], target)
    arrived(final.at[0, 0 : zs - 1], red_recv.at[4])
    send(final.at[core], final.at[core], red_send, red_recv.at[5], (sibling, h))
    arrived(final.at[0], red_recv.at[5])
    for c in range(2):
        for zz in range(zs):
            first = c * BLOCK + zz * chunk
            for yy in range(ys):
                pg_ref[first : first + chunk, yy * width : (yy + 1) * width] = final[c, zz, yy].astype(F32)

    arrived(ext.at[: 2 * BLOCK], row_send)
    arrived(lv1, row_send)
    arrived(up, row_send)
    arrived(gext, grad_send)
    arrived(gu, grad_send)
    if heads > 1:
        arrived(gfull.at[0 : heads - 1], x_send)
        arrived(got_part, x_send)
    arrived(got_half, red_send)
    arrived(got_z, red_send)
    arrived(got_y, red_send)
    arrived(got_y, red_send)
    arrived(final.at[0, 0 : zs - 1], red_send)
    arrived(final.at[0], red_send)


def body(zs, ys, queries, keys, values, grad_out, proj_weight):
    devices = lax.axis_size("seq")
    heads = lax.axis_size("head")
    model = proj_weight.shape[1]
    chunk, width = BLOCK // zs, model // ys
    vmem = pl.BlockSpec(memory_space=pltpu.VMEM)
    wide = 2 * FEAT
    scratch = [
        ((4 * BLOCK, wide), BF16),
        ((4 * HALF, wide), BF16),
        ((240, wide), BF16),
        ((UPPER, wide), BF16),
        ((heads, ROWS, FEAT), BF16),
        ((4 * BLOCK, wide), BF16),
        ((4 * HALF, wide), F32),
        ((UPPER, wide), BF16),
        ((2, BLOCK, wide), BF16),
        ((2, BLOCK, wide), BF16),
        ((3, HALF, wide), BF16),
        ((6, HALF // 2, wide), BF16),
        ((12, HALF // 4, wide), BF16),
        ((heads, ROWS, FEAT), BF16),
        ((max(heads - 1, 1), ROWS, FEAT), BF16),
        ((HEADS_HERE, 2, OWN_KEYS, BLOCK), F32),
        ((HEADS_HERE, UPPER, ROWS), F32),
        ((ROWS, wide), F32),
        ((2, BLOCK, model), F32),
        ((2, BLOCK, model), BF16),
        ((BLOCK, model), BF16),
        ((zs, chunk, model), BF16),
        ((zs - 1, chunk, model), BF16),
        ((ys, chunk, width), BF16),
        ((ys - 1, chunk, width), BF16),
        ((2, zs, ys, chunk, width), BF16),
    ]
    like = jax.ShapeDtypeStruct
    return pl.pallas_call(
        functools.partial(kernel, devices, heads, zs, ys),
        out_shape=(
            like((ROWS, FEAT), BF16),
            like((ROWS, FEAT), BF16),
            like((ROWS, FEAT), BF16),
            like((ROWS, FEAT), BF16),
            like((FEAT, model), F32),
        ),
        in_specs=[vmem] * 5,
        out_specs=[vmem] * 5,
        scratch_shapes=[pltpu.VMEM(shape, kind) for shape, kind in scratch]
        + [
            pltpu.SemaphoreType.DMA,
            pltpu.SemaphoreType.DMA((5,)),
            pltpu.SemaphoreType.DMA,
            pltpu.SemaphoreType.DMA((5,)),
            pltpu.SemaphoreType.DMA,
            pltpu.SemaphoreType.DMA((2,)),
            pltpu.SemaphoreType.DMA,
            pltpu.SemaphoreType.DMA((6,)),
        ],
        compiler_params=pltpu.CompilerParams(
            collective_id=0, has_side_effects=True, vmem_limit_bytes=40 * 1024 * 1024
        ),
        name="attention",
    )(queries, keys, values, grad_out, proj_weight)


def solution(mesh):
    devices = mesh.shape["seq"]
    zs = 8 if devices == 128 else 2
    ys = devices // (2 * zs)
    spec = P("seq", "head")
    return jax.shard_map(
        functools.partial(body, zs, ys),
        mesh=mesh,
        in_specs=(spec, spec, spec, spec, P("head", None)),
        out_specs=(spec, spec, spec, spec, P("head", None)),
        check_vma=False,
    )
```

time: 413 us -> 81.1 us (0.20)
  waiting for transfers between devices: 151 us -> 0 us
  starting transfers between devices: 138 us -> 0 us
  Pallas kernels: 0 us -> 72 us
  local copies, waits for them, and re-layouts: 52.1 us -> 8.24 us
  matrix products: 25.6 us -> 0 us
  between operations: 17.4 us -> 0.66 us
  other arithmetic: 13.1 us -> 0 us
  blocking collectives: 11.3 us -> 0 us
    psum x1 -> x0, waiting for transfers between devices: 144 us -> none  [body(): lax.psum(jnp.einsum('tw,td->wd', attended, grad_full, preferred_element_t...]
    ppermute x40 -> x0, starting transfers between devices: 138 us -> none  [the longest x36 118 us: from_behind(): return lax.ppermute(block, axis, route)]
    pallas_call x0 -> x1, Pallas kernels: none -> 72 us  [body(): pl.pallas_call(functools.partial(kernel, devices, heads, zs, ys), out_sha...]
    dot_general x33 -> x0, matrix products: 25.6 us -> none  [the longest x5 5.91 us: body(): jnp.einsum('grhk,gkhd->grhd', weights, value_view, preferred_element_type...]
    slice x24 -> x0, local copies, waits for them, and re-layouts: 15.8 us -> none  [the longest x8 8.49 us: body(): keyset[:, :, feat_width:].reshape(group_count, -1, heads_here, HEAD_DIM)]
    reshape x20 -> x0, local copies, waits for them, and re-layouts: 15.5 us -> none  [the longest x3 4.7 us: body(): attended32 = attended32 + jnp.einsum('grhk,gkhd->grhd', weights, value_vi...]
    all_gather x1 -> x0, blocking collectives: 11.3 us -> none  [body(): grad_full = lax.all_gather(grad_out, 'head', axis=1, tiled=True)]
    ppermute x40 -> x0, waiting for transfers between devices: 7.48 us -> none  [the longest x36 5.82 us: from_behind(): return lax.ppermute(block, axis, route)]
  transfers between devices with their start and end apart: 42 -> 0, of which waited for: 4 -> 0; matrix products, arithmetic and copies ran while one was open for 11% -> 0% of each run, Pallas kernels for 0% -> 0%
where the time goes in v1:
time: 81.1 us; the launch traced here: 80.9 us
  Pallas kernels  72 us (89%)
  local copies, waits for them, and re-layouts  8.24 us (10%)
    pallas_call x1, Pallas kernels, body(): pl.pallas_call(functools.partial(kernel, devices, heads, zs, ys), out_sha...  72 us
    unnamed x15, local copies, waits for them, and re-layouts  8.24 us

profile of v1, /device:TPU:1, one launch (start us, length us, event | category | flops | bytes accessed | tf_op | source)
XLA Modules:
  0.0 80.9 jit_solution(12025057717725170035)
XLA Ops:
  0.6 0.0 copy-start
  0.6 1.0 %copy-done = bf16[256,1024]{1,0:T(8,128)(2,1)S(1)} copy-done((bf16[256,1024]{1,0:T(8,128)(2,1)S(1)}, bf16[256,1024]{1,0:T(8,128)(2,1)}, u32[]{:S(2)}) %copy-start) | copy-done | bytes 524312
  1.7 0.0 copy-start.1
  1.7 0.9 %copy-done.1 = bf16[256,256]{1,0:T(8,128)(2,1)S(1)} copy-done((bf16[256,256]{1,0:T(8,128)(2,1)S(1)}, bf16[256,256]{1,0:T(8,128)(2,1)}, u32[]{:S(2)}) %copy-start.1) | copy-done | bytes 131096
  2.6 0.0 copy-start.2
  2.6 0.9 %copy-done.2 = bf16[256,256]{1,0:T(8,128)(2,1)S(1)} copy-done((bf16[256,256]{1,0:T(8,128)(2,1)S(1)}, bf16[256,256]{1,0:T(8,128)(2,1)}, u32[]{:S(2)}) %copy-start.2) | copy-done | bytes 131096
  3.5 0.0 copy-start.3
  3.5 0.9 %copy-done.3 = bf16[256,256]{1,0:T(8,128)(2,1)S(1)} copy-done((bf16[256,256]{1,0:T(8,128)(2,1)S(1)}, bf16[256,256]{1,0:T(8,128)(2,1)}, u32[]{:S(2)}) %copy-start.3) | copy-done | bytes 131096
  4.4 0.0 copy-start.4
  4.4 0.9 %copy-done.4 = bf16[256,256]{1,0:T(8,128)(2,1)S(1)} copy-done((bf16[256,256]{1,0:T(8,128)(2,1)S(1)}, bf16[256,256]{1,0:T(8,128)(2,1)}, u32[]{:S(2)}) %copy-start.4) | copy-done | bytes 131096
  5.3 72.0 %attention.1 = (bf16[256,256]{1,0:T(8,128)(2,1)S(1)}, bf16[256,256]{1,0:T(8,128)(2,1)S(1)}, bf16[256,256]{1,0:T(8,128)(2,1)S(1)}, bf16[256,256]{1,0:T(8,128)(2,1)S(1)}, f32[256,1024]{1,0:T(8,128)S(1)}) custom-call(bf16[256,256]{1,0:T(8,128)(2,1)S(1)} %copy-done.1, bf16[256,256]{1,0:T(8,128)(2,1)S(1)} %copy-done.2, bf16[256,256]{1,0:T(8,128)(2,1)S(1)} %copy-done.3, ...), custom_call_target="tpu_custom_call" | custom-call | tf_op jit(solution)/shard_map/attention/pallas_call | solution.py:407
  77.3 0.7 copy.15
  77.9 0.7 copy.16
  78.6 0.7 copy.17
  79.2 0.7 copy.18
  79.9 1.0 %copy.19 = f32[256,1024]{1,0:T(8,128)} copy(f32[256,1024]{1,0:T(8,128)S(1)} %get-tuple-element.14) | data formatting | bytes 2097152
Async XLA Ops:
  0.6 1.0 %copy-start = (bf16[256,1024]{1,0:T(8,128)(2,1)S(1)}, bf16[256,1024]{1,0:T(8,128)(2,1)}, u32[]{:S(2)}) copy-start(bf16[256,1024]{1,0:T(8,128)(2,1)} %w_ref.1) | copy-start | bytes 1572868
  1.7 0.9 %copy-start.1 = (bf16[256,256]{1,0:T(8,128)(2,1)S(1)}, bf16[256,256]{1,0:T(8,128)(2,1)}, u32[]{:S(2)}) copy-start(bf16[256,256]{1,0:T(8,128)(2,1)} %q_ref.1) | copy-start | bytes 393220
  2.6 0.9 %copy-start.2 = (bf16[256,256]{1,0:T(8,128)(2,1)S(1)}, bf16[256,256]{1,0:T(8,128)(2,1)}, u32[]{:S(2)}) copy-start(bf16[256,256]{1,0:T(8,128)(2,1)} %k_ref.1) | copy-start | bytes 393220
  3.5 0.9 %copy-start.3 = (bf16[256,256]{1,0:T(8,128)(2,1)S(1)}, bf16[256,256]{1,0:T(8,128)(2,1)}, u32[]{:S(2)}) copy-start(bf16[256,256]{1,0:T(8,128)(2,1)} %v_ref.1) | copy-start | bytes 393220
  4.4 0.9 %copy-start.4 = (bf16[256,256]{1,0:T(8,128)(2,1)S(1)}, bf16[256,256]{1,0:T(8,128)(2,1)}, u32[]{:S(2)}) copy-start(bf16[256,256]{1,0:T(8,128)(2,1)} %go_ref.1) | copy-start | bytes 393220

commit v2 on v1

v2 whole, which is shorter than its diff:
```python
import functools
import math

import jax
import jax.numpy as jnp
from jax import lax
from jax.experimental import pallas as pl
from jax.experimental.pallas import tpu as pltpu
from jax.sharding import PartitionSpec as P

HEAD_DIM = 128
BLOCK = 128
HALF = BLOCK // 2
ROWS = 256
FEAT = 256
HEADS_HERE = FEAT // HEAD_DIM
NEAR = 3 * BLOCK
OWN_KEYS = NEAR + 3 * HALF
UPPER = 9 * HALF
PART = 3 * 32 + 6 * 16
NEG = -1e30
SCALE = 1.0 / math.sqrt(HEAD_DIM)
EXP2_SCALE = SCALE * math.log2(math.e)
MESH = pl.DeviceIdType.MESH
F32 = jnp.float32
BF16 = jnp.bfloat16


def dot(a, b):
    return lax.dot_general(a, b, (((1,), (0,)), ((), ())), preferred_element_type=F32)


def dot_nt(a, b):
    return lax.dot_general(a, b, (((1,), (1,)), ((), ())), preferred_element_type=F32)


def dot_tn(a, b):
    return lax.dot_general(a, b, (((0,), (0,)), ((), ())), preferred_element_type=F32)


def pair_average(rows):
    row = lax.broadcasted_iota(jnp.int32, (rows // 2, rows), 0)
    column = lax.broadcasted_iota(jnp.int32, (rows // 2, rows), 1)
    return jnp.where((column >= 2 * row) & (column < 2 * row + 2), 0.5, 0.0).astype(BF16)


def spread_matrix():
    parts = []
    for level in range(1, 5):
        count = ROWS >> level
        token = lax.broadcasted_iota(jnp.int32, (ROWS, count), 0)
        first = lax.broadcasted_iota(jnp.int32, (ROWS, count), 1) * (1 << level)
        inside = (token >= first) & (token < first + (1 << level))
        parts.append(jnp.where(inside, 0.5**level, 0.0).astype(BF16))
    return parts


def kernel(
    devices, heads, zs, ys,
    q_in, k_in, v_in, go_in, w_in,
    proj_ref, dq_ref, dk_ref, dv_ref, final,
    q_ref, w_ref, ext, lv1, own, up, gfull,
    edge, e_near, g1, near_out, gu, from_sib, gsum, from_mate, got_near, got2, got3, got4,
    part, got_part, s_own, s_up, pg32, pg16, got_half, mine, got_z, cross, got_y,
    in_sem, row_send, row_recv, grad_send, grad_recv, x_send, x_recv, red_send, red_recv, last_recv,
):
    d = lax.axis_index("seq")
    h = lax.axis_index("head")
    core = lax.rem(d, 2)
    y = lax.rem(d // 2, ys)
    z = d // (2 * ys)
    chip = d // 2
    quad = d // 4
    side = lax.rem(chip, 2)

    def at(target):
        return (lax.rem(target + 2 * devices, devices), h)

    def send(src, dst, send_sem, recv_sem, target):
        copy = pltpu.make_async_remote_copy(
            src_ref=src, dst_ref=dst, send_sem=send_sem, recv_sem=recv_sem,
            device_id=target, device_id_type=MESH,
        )
        copy.start()

    def arrived(ref, sem):
        pltpu.make_async_copy(ref, ref, sem).wait()

    def rows_of(ref, first, count):
        return ref.at[pl.ds(pl.multiple_of(first, 16), count)]

    def far(index, total):
        wide = 3 - 6 * lax.rem(index, 2)
        return [lax.rem(index + o + total, total) for o in (2, -2, wide)]

    sibling = (d + 1 - 2 * core, h)
    mate = (4 * quad + 2 * (1 - side) + core, h)
    left, right = at(d - 1), at(d + 1)
    two = [at(d + 2), at(d - 2)]
    three = [(2 * t + core, h) for t in far(chip, devices // 2)]
    four = [(4 * t + 2 * (1 - side) + core, h) for t in far(quad, devices // 4)]
    across = [(d, lax.rem(h + r, heads)) for r in range(1, heads)]

    def z_peer(r):
        return lax.rem(z + r, zs) * (2 * ys) + 2 * y + core

    def y_peer(r):
        return z * (2 * ys) + 2 * lax.rem(y + r, ys) + core

    z_peers = [(z_peer(r), h) for r in range(1, zs)]
    y_peers = [(y_peer(r), h) for r in range(1, ys)]

    barrier = pltpu.get_barrier_semaphore()
    everyone = [left, right, mate, *two, *three, *four, *across, *z_peers, *y_peers]
    for target in everyone:
        pl.semaphore_signal(barrier, inc=1, device_id=target, device_id_type=MESH)

    own_rows = ext.at[BLOCK : BLOCK + ROWS]
    loads = [
        (k_in, own_rows.at[:, :FEAT]), (v_in, own_rows.at[:, FEAT:]),
        (go_in, gfull.at[h]), (q_in, q_ref), (w_in, w_ref),
    ]
    loads = [pltpu.make_async_copy(src, dst, in_sem.at[i]) for i, (src, dst) in enumerate(loads)]
    for load in loads:
        load.start()
    loads[0].wait()
    loads[1].wait()

    rows = ext[BLOCK : BLOCK + ROWS]
    offset = 0
    for level in range(1, 5):
        rows = dot(pair_average(rows.shape[0]), rows).astype(BF16)
        own[offset : offset + rows.shape[0]] = rows
        offset += rows.shape[0]
    for load in loads[2:]:
        load.wait()
    pl.semaphore_wait(barrier, len(everyone))

    mine_part = 3 * HALF + core * PART
    for slot in range(3):
        dst = rows_of(up, mine_part + 96 + side * 48 + slot * 16, 16)
        send(own.at[224:240], dst, row_send, row_recv.at[4], four[slot])
    for slot in range(3):
        dst = rows_of(up, mine_part + slot * 32, 32)
        send(own.at[192:224], dst, row_send, row_recv.at[3], three[slot])
    for slot in range(2):
        send(own.at[128:192], up.at[slot * HALF : (slot + 1) * HALF], row_send, row_recv.at[2], two[slot])
    send(ext.at[BLOCK : 2 * BLOCK], ext.at[3 * BLOCK :], row_send, row_recv.at[0], left)
    send(ext.at[2 * BLOCK : 3 * BLOCK], ext.at[:BLOCK], row_send, row_recv.at[0], right)
    send(own.at[HALF : 2 * HALF], lv1.at[2 * HALF : 3 * HALF], row_send, row_recv.at[1], left)
    send(own.at[:HALF], lv1.at[HALF : 2 * HALF], row_send, row_recv.at[1], right)
    for target in across:
        send(gfull.at[h], gfull.at[h], x_send, x_recv.at[0], target)

    taken = rows_of(up, mine_part + 96 + (1 - side) * 48, 48)
    arrived(taken, row_recv.at[4])
    send(taken, taken, row_send, row_recv.at[5], mate)
    send(taken, taken, row_send, row_recv.at[6], sibling)
    level3 = rows_of(up, mine_part, 96)
    arrived(level3, row_recv.at[3])
    send(level3, level3, row_send, row_recv.at[6], sibling)
    arrived(up.at[: 2 * HALF], row_recv.at[2])
    send(rows_of(up, core * HALF, HALF), up.at[2 * HALF : 3 * HALF], row_send, row_recv.at[6], sibling)
    handed = rows_of(up, mine_part + 96 + side * 48, 48)
    arrived(handed, row_recv.at[5])
    send(handed, handed, row_send, row_recv.at[6], sibling)

    def bias(valid):
        return jnp.where(valid, 0.0, NEG).astype(F32)

    left_bias, right_bias = bias(d >= 1), bias(d <= devices - 2)

    def far_bias(index, total):
        wide = index + 3 - 6 * lax.rem(index, 2)
        return [bias(index >= 2), bias(index + 2 < total), bias((wide >= 0) & (wide < total))]

    bias2, bias3, bias4 = far_bias(d, devices), far_bias(chip, devices // 2), far_bias(quad, devices // 4)
    up_bias = [(HALF, b) for b in bias2]
    for _ in range(2):
        up_bias += [(32, b) for b in bias3] + [(16, b) for b in bias4 + bias4]

    def head_cols(head):
        return slice(head * HEAD_DIM, (head + 1) * HEAD_DIM)

    def value_cols(head):
        return slice(FEAT + head * HEAD_DIM, FEAT + (head + 1) * HEAD_DIM)

    def block_keys(block, cols):
        near = ext[block * BLOCK : block * BLOCK + NEAR, cols]
        return jnp.concatenate([near, lv1[block * HALF : block * HALF + 3 * HALF, cols]], axis=0)

    def block_queries(block, head):
        return q_ref[block * BLOCK : (block + 1) * BLOCK, head_cols(head)]

    arrived(ext.at[: 2 * BLOCK], row_recv.at[0])
    lv1[:HALF] = dot(pair_average(BLOCK), ext[3 * BLOCK :]).astype(BF16)
    lv1[3 * HALF :] = dot(pair_average(BLOCK), ext[:BLOCK]).astype(BF16)
    arrived(lv1.at[: 2 * HALF], row_recv.at[1])
    own_peak = [[None] * 2 for _ in range(HEADS_HERE)]
    for head in range(HEADS_HERE):
        for block in range(2):
            scores = dot_nt(block_keys(block, head_cols(head)), block_queries(block, head))
            if block == 0:
                pieces = [
                    scores[:BLOCK] + left_bias,
                    scores[BLOCK:NEAR],
                    scores[NEAR : NEAR + HALF] + right_bias,
                    scores[NEAR + HALF : NEAR + 2 * HALF] + left_bias,
                    scores[NEAR + 2 * HALF :] + right_bias,
                ]
            else:
                pieces = [
                    scores[: 2 * BLOCK],
                    scores[2 * BLOCK : NEAR] + right_bias,
                    scores[NEAR : NEAR + HALF] + left_bias,
                    scores[NEAR + HALF : NEAR + 2 * HALF] + right_bias,
                    scores[NEAR + 2 * HALF :] + left_bias,
                ]
            scores = jnp.concatenate(pieces, axis=0)
            s_own[head, block] = scores
            own_peak[head][block] = scores.max(axis=0, keepdims=True)

    if heads > 1:
        arrived(gfull.at[0 : heads - 1], x_recv.at[0])
    grad_full = jnp.concatenate([gfull[r] for r in range(heads)], axis=1)
    grad = dot_nt(grad_full, w_ref[...]).astype(BF16)
    grad_t = dot_nt(w_ref[...], grad_full).astype(BF16)

    arrived(up.at[: HALF + PART], row_recv.at[6])
    att_t = []
    for head in range(HEADS_HERE):
        raw = dot_nt(up[:, head_cols(head)], q_ref[:, head_cols(head)])
        pieces, first = [], 0
        for count, piece_bias in up_bias:
            pieces.append(raw[first : first + count] + piece_bias)
            first += count
        raw = jnp.concatenate(pieces, axis=0)
        peak = jnp.maximum(jnp.concatenate(own_peak[head], axis=1), raw.max(axis=0, keepdims=True))
        lifted_up = jnp.exp2((raw - peak) * EXP2_SCALE)
        total = lifted_up.sum(axis=0, keepdims=True)
        own_total = []
        for block in range(2):
            block_peak = peak[:, block * BLOCK : (block + 1) * BLOCK]
            lifted = jnp.exp2((s_own[head, block] - block_peak) * EXP2_SCALE)
            s_own[head, block] = lifted
            own_total.append(lifted.sum(axis=0, keepdims=True))
        inv = 1.0 / (total + jnp.concatenate(own_total, axis=1))
        prob_up = lifted_up * inv
        s_up[head] = prob_up
        up_att = dot_tn(up[:, value_cols(head)], prob_up.astype(BF16))
        own_att = []
        for block in range(2):
            prob = s_own[head, block] * inv[:, block * BLOCK : (block + 1) * BLOCK]
            s_own[head, block] = prob
            own_att.append(dot_tn(block_keys(block, value_cols(head)), prob.astype(BF16)))
        att_t.append(up_att + jnp.concatenate(own_att, axis=1))
    att16_t = jnp.concatenate(att_t, axis=0).astype(BF16)

    for c in range(2):
        half = dot(att16_t[c * BLOCK : (c + 1) * BLOCK], grad_full)
        pg32[c] = half
        pg16[c] = half.astype(BF16)
    send(pg16.at[1 - core], got_half, red_send, red_recv.at[0], sibling)

    delta = []
    dq_t = []
    for head in range(HEADS_HERE):
        g_t = grad_t[head_cols(head)]
        delta.append((g_t.astype(F32) * att_t[head]).sum(axis=0, keepdims=True))
        prob = s_up[head]
        dprob = dot(up[:, value_cols(head)], g_t)
        dscore = (prob * (dprob - delta[head]) * SCALE).astype(BF16)
        dq_t.append(dot_tn(up[:, head_cols(head)], dscore))
        gu[:, head_cols(head)] = dot(dscore, q_ref[:, head_cols(head)]).astype(BF16)
        gu[:, value_cols(head)] = dot(prob.astype(BF16), grad[:, head_cols(head)]).astype(BF16)
    send(rows_of(gu, 3 * HALF + (1 - core) * PART, PART), from_sib.at[HALF:], grad_send, grad_recv.at[5], sibling)
    send(gu.at[2 * HALF : 3 * HALF], from_sib.at[:HALF], grad_send, grad_recv.at[5], sibling)

    arrived(got_half, red_recv.at[0])
    chunk = BLOCK // zs
    for i in range(zs):
        window = slice(i * chunk, (i + 1) * chunk)
        mine[i] = (pg32[core, window] + got_half[window].astype(F32)).astype(BF16)
    for r, target in enumerate(z_peers):
        send(mine.at[lax.rem(z + r + 1, zs)], got_z.at[r], red_send, red_recv.at[1], target)

    arrived(from_sib, grad_recv.at[5])
    gsum[2 * HALF :] = (gu[pl.ds(pl.multiple_of(mine_part, 16), PART)].astype(F32) + from_sib[HALF:].astype(F32)).astype(BF16)
    send(rows_of(gsum, 2 * HALF + 96 + side * 48, 48), from_mate, grad_send, grad_recv.at[6], mate)
    for slot in range(3):
        src = gsum.at[2 * HALF + slot * 32 : 2 * HALF + (slot + 1) * 32]
        send(src, got3.at[slot], grad_send, grad_recv.at[3], three[(1, 0, 2)[slot]])
    gsum[: 2 * HALF] = gu[: 2 * HALF]
    shared = pl.ds(pl.multiple_of(core * HALF, 16), HALF)
    gsum[shared] = (gu[shared].astype(F32) + from_sib[:HALF].astype(F32)).astype(BF16)
    for slot in range(2):
        src = gsum.at[slot * HALF : (slot + 1) * HALF]
        send(src, got2.at[slot], grad_send, grad_recv.at[2], two[1 - slot])

    for head in range(HEADS_HERE):
        own_dq = []
        for block in range(2):
            cols = slice(block * BLOCK, (block + 1) * BLOCK)
            prob = s_own[head, block]
            dprob = dot(block_keys(block, value_cols(head)), grad_t[head_cols(head), cols])
            dscore = (prob * (dprob - delta[head][:, cols]) * SCALE).astype(BF16)
            own_dq.append(dot_tn(block_keys(block, head_cols(head)), dscore))
            dkey = dot(dscore, block_queries(block, head))
            dval = dot(prob.astype(BF16), grad[cols, head_cols(head)])
            for grads, column in ((dkey, head_cols(head)), (dval, value_cols(head))):
                if block == 0:
                    edge[0, :, column] = grads[:BLOCK]
                    e_near[:, column] = grads[BLOCK:NEAR]
                    g1[: 3 * HALF, column] = grads[NEAR:]
                else:
                    e_near[:, column] = e_near[:, column] + grads[: 2 * BLOCK]
                    edge[1, :, column] = grads[2 * BLOCK : NEAR]
                    g1[HALF : 3 * HALF, column] = g1[HALF : 3 * HALF, column] + grads[NEAR : NEAR + 2 * HALF]
                    g1[3 * HALF :, column] = grads[NEAR + 2 * HALF :]
        dq_t[head] = dq_t[head] + jnp.concatenate(own_dq, axis=1)
    levels = spread_matrix()
    pairs = levels[0][:BLOCK, :HALF]
    near_out[0, :BLOCK] = (edge[0] + dot(pairs, g1[3 * HALF :].astype(BF16))).astype(BF16)
    near_out[0, BLOCK:] = g1[HALF : 2 * HALF].astype(BF16)
    near_out[1, :BLOCK] = (edge[1] + dot(pairs, g1[:HALF].astype(BF16))).astype(BF16)
    near_out[1, BLOCK:] = g1[2 * HALF : 3 * HALF].astype(BF16)
    send(near_out.at[0], got_near.at[1], grad_send, grad_recv.at[0], left)
    send(near_out.at[1], got_near.at[0], grad_send, grad_recv.at[0], right)

    arrived(from_mate, grad_recv.at[6])
    kept = pl.ds(pl.multiple_of(2 * HALF + 96 + (1 - side) * 48, 16), 48)
    gsum[kept] = (gsum[kept].astype(F32) + from_mate[...].astype(F32)).astype(BF16)
    for slot in range(3):
        src = rows_of(gsum, 2 * HALF + 96 + (1 - side) * 48 + slot * 16, 16)
        send(src, got4.at[slot], grad_send, grad_recv.at[4], four[(1, 0, 2)[slot]])

    arrived(got_z, red_recv.at[1])
    total = mine[z].astype(F32)
    for r in range(zs - 1):
        total = total + got_z[r].astype(F32)
    width = cross.shape[2]
    for i in range(ys):
        cross[i] = total[:, i * width : (i + 1) * width].astype(BF16)
    for r, target in enumerate(y_peers):
        send(cross.at[lax.rem(y + r + 1, ys)], got_y.at[r], red_send, red_recv.at[2], target)

    partial = dot(att16_t.T, w_ref[...])
    for r in range(heads):
        part[r] = partial[:, r * FEAT : (r + 1) * FEAT].astype(BF16)
    for r, target in enumerate(across):
        send(part.at[target[1]], got_part.at[r], x_send, x_recv.at[1], target)
    dq_ref[...] = jnp.concatenate(dq_t, axis=0).T.astype(BF16)

    arrived(got_y, red_recv.at[2])
    total = cross[y].astype(F32)
    for r in range(ys - 1):
        total = total + got_y[r].astype(F32)
    swap = core == 1
    first, second = jnp.where(swap, z, y), jnp.where(swap, y, z)
    block = final.at[core, second, first]
    final[core, second, first] = total.astype(BF16)
    for r in range(1, ys):
        send(block, block, red_send, red_recv.at[3], (jnp.where(swap, z_peer(r), y_peer(r)), h))
    arrived(got_y, red_recv.at[3])
    line = final.at[core, second]
    for r in range(1, zs):
        send(line, line, red_send, last_recv.at[r - 1], (jnp.where(swap, y_peer(r), z_peer(r)), h))
    send(line, line, red_send, red_recv.at[4], sibling)

    if heads > 1:
        arrived(got_part, x_recv.at[1])
    projected = part[h].astype(F32)
    for r in range(heads - 1):
        projected = projected + got_part[r].astype(F32)
    proj_ref[...] = projected.astype(BF16)

    arrived(got4, grad_recv.at[4])
    arrived(got3, grad_recv.at[3])
    arrived(got2, grad_recv.at[2])
    arrived(got_near, grad_recv.at[0])
    rows_grad = e_near[...] + jnp.concatenate([got_near[0, :BLOCK], got_near[1, :BLOCK]], axis=0).astype(F32)
    rows_grad = rows_grad + dot(levels[0], jnp.concatenate([got_near[1, BLOCK:], got_near[0, BLOCK:]], axis=0))
    for level, got in ((1, got2), (2, got3), (3, got4)):
        total = got[0].astype(F32)
        for i in range(1, got.shape[0]):
            total = total + got[i].astype(F32)
        rows_grad = rows_grad + dot(levels[level], total.astype(BF16))
    dk_ref[...] = rows_grad[:, :FEAT].astype(BF16)
    dv_ref[...] = rows_grad[:, FEAT:].astype(BF16)

    for r in range(1, zs):
        arrived(line, last_recv.at[r - 1])
        piece = final.at[core, lax.rem(second + zs - r, zs)]
        send(piece, piece, red_send, red_recv.at[4], sibling)
    arrived(final.at[0], red_recv.at[4])

    arrived(up.at[: 48 + 96 + 2 * HALF], row_send)
    arrived(up.at[: 2 * BLOCK + 2 * HALF], row_send)
    arrived(up.at[: 48 + HALF + PART], row_send)
    arrived(from_sib, grad_send)
    arrived(up.at[: 48 + 96 + 2 * HALF + 48], grad_send)
    arrived(near_out, grad_send)
    if heads > 1:
        arrived(gfull.at[0 : heads - 1], x_send)
        arrived(got_part, x_send)
    arrived(got_half, red_send)
    arrived(got_z, red_send)
    arrived(got_y, red_send)
    arrived(got_y, red_send)
    arrived(final.at[0, 0 : zs - 1], red_send)
    arrived(final.at[0], red_send)


def finish(proj, dq, dk, dv, final, proj_out, dq_out, dk_out, dv_out, pg_out, pg, sems):
    small = ((proj, proj_out), (dq, dq_out), (dk, dk_out), (dv, dv_out))
    copies = [pltpu.make_async_copy(src, dst, sems.at[i]) for i, (src, dst) in enumerate(small)]
    for copy in copies:
        copy.start()
    _, zs, ys, chunk, width = final.shape
    for c in range(2):
        for zz in range(zs):
            first = c * BLOCK + zz * chunk
            for yy in range(ys):
                piece = final[0, zz, yy] if c == 0 else final[1, yy, zz]
                pg[first : first + chunk, yy * width : (yy + 1) * width] = piece.astype(F32)
        half = slice(c * BLOCK, (c + 1) * BLOCK)
        copies.append(pltpu.make_async_copy(pg.at[half], pg_out.at[half], sems.at[4 + c]))
        copies[-1].start()
    for copy in copies:
        copy.wait()


def body(zs, ys, queries, keys, values, grad_out, proj_weight):
    devices = lax.axis_size("seq")
    heads = lax.axis_size("head")
    model = proj_weight.shape[1]
    chunk, width = BLOCK // zs, model // ys
    vmem = pl.BlockSpec(memory_space=pltpu.VMEM)
    hbm = pl.BlockSpec(memory_space=pltpu.HBM)
    wide = 2 * FEAT
    scratch = [
        ((ROWS, FEAT), BF16),
        ((FEAT, model), BF16),
        ((4 * BLOCK, wide), BF16),
        ((4 * HALF, wide), BF16),
        ((240, wide), BF16),
        ((UPPER, wide), BF16),
        ((heads, ROWS, FEAT), BF16),
        ((2, BLOCK, wide), F32),
        ((ROWS, wide), F32),
        ((4 * HALF, wide), F32),
        ((2, BLOCK + HALF, wide), BF16),
        ((UPPER, wide), BF16),
        ((HALF + PART, wide), BF16),
        ((2 * HALF + PART, wide), BF16),
        ((48, wide), BF16),
        ((2, BLOCK + HALF, wide), BF16),
        ((2, HALF, wide), BF16),
        ((3, HALF // 2, wide), BF16),
        ((3, HALF // 4, wide), BF16),
        ((heads, ROWS, FEAT), BF16),
        ((max(heads - 1, 1), ROWS, FEAT), BF16),
        ((HEADS_HERE, 2, OWN_KEYS, BLOCK), F32),
        ((HEADS_HERE, UPPER, ROWS), F32),
        ((2, BLOCK, model), F32),
        ((2, BLOCK, model), BF16),
        ((BLOCK, model), BF16),
        ((zs, chunk, model), BF16),
        ((zs - 1, chunk, model), BF16),
        ((ys, chunk, width), BF16),
        ((ys - 1, chunk, width), BF16),
    ]
    like = jax.ShapeDtypeStruct
    dma = pltpu.SemaphoreType.DMA
    small = like((ROWS, FEAT), BF16)
    results = pl.pallas_call(
        functools.partial(kernel, devices, heads, zs, ys),
        out_shape=(small, small, small, small, like((2, zs, ys, chunk, width), BF16)),
        in_specs=[hbm] * 5,
        out_specs=[vmem] * 5,
        scratch_shapes=[pltpu.VMEM(shape, kind) for shape, kind in scratch]
        + [dma((5,)), dma, dma((7,)), dma, dma((7,)), dma, dma((2,)), dma, dma((5,)), dma((zs - 1,))],
        compiler_params=pltpu.CompilerParams(
            collective_id=0, has_side_effects=True, vmem_limit_bytes=63 * 1024 * 1024
        ),
        name="attention",
    )(queries, keys, values, grad_out, proj_weight)
    return pl.pallas_call(
        finish,
        out_shape=(small, small, small, small, like((FEAT, model), F32)),
        in_specs=[vmem] * 5,
        out_specs=[hbm] * 5,
        scratch_shapes=[pltpu.VMEM((FEAT, model), F32), dma((6,))],
        name="finish",
    )(*results)


def solution(mesh):
    devices = mesh.shape["seq"]
    zs = math.isqrt(devices // 2)
    ys = devices // (2 * zs)
    spec = P("seq", "head")
    return jax.shard_map(
        functools.partial(body, zs, ys),
        mesh=mesh,
        in_specs=(spec, spec, spec, spec, P("head", None)),
        out_specs=(spec, spec, spec, spec, P("head", None)),
        check_vma=False,
    )
```

time: 81.1 us -> 66.6 us (0.82)
  local copies, waits for them, and re-layouts: 8.24 us -> 0 us
  Pallas kernels: 72 us -> 65.8 us
    pallas_call x1, Pallas kernels: 72 us -> 63.3 us  [body(): pl.pallas_call(functools.partial(kernel, devices, heads, zs, ys), out_sha...]
    unnamed x15 -> x0, local copies, waits for them, and re-layouts: 8.24 us -> none
    pallas_call x0 -> x1, Pallas kernels: none -> 2.5 us  [body(): pl.pallas_call(finish, out_shape=(small, small, small, small, like((FEAT,...]
where the time goes in v2:
time: 66.6 us; the launch traced here: 66.4 us
  Pallas kernels  65.8 us (99%)
    pallas_call x1, Pallas kernels, body(): pl.pallas_call(functools.partial(kernel, devices, heads, zs, ys), out_sha...  63.3 us
    pallas_call x1, Pallas kernels, body(): pl.pallas_call(finish, out_shape=(small, small, small, small, like((FEAT,...  2.5 us

profile of v2, /device:TPU:1, one launch (start us, length us, event | category | flops | bytes accessed | tf_op | source)
XLA Modules:
  0.0 66.4 jit_solution(3396611923205530115)
XLA Ops:
  0.6 63.3 %attention.1 = (bf16[256,256]{1,0:T(8,128)(2,1)}, bf16[256,256]{1,0:T(8,128)(2,1)}, bf16[256,256]{1,0:T(8,128)(2,1)}, bf16[256,256]{1,0:T(8,128)(2,1)}, bf16[2,8,8,16,128]{4,3,2,1,0:T(8,128)(2,1)}) custom-call(bf16[256,256]{1,0:T(8,128)(2,1)} %q_in.1, bf16[256,256]{1,0:T(8,128)(2,1)} %k_in.1, bf16[256,256]{1,0:T(8,128)(2,1)} %v_in.1, ...), custom_call_target="tpu_custom_call" | custom-call | tf_op jit(solution)/shard_map/attention/pallas_call | solution.py:476
  63.9 2.5 %finish.1 = (bf16[256,256]{1,0:T(8,128)(2,1)}, bf16[256,256]{1,0:T(8,128)(2,1)}, bf16[256,256]{1,0:T(8,128)(2,1)}, bf16[256,256]{1,0:T(8,128)(2,1)}, f32[256,1024]{1,0:T(8,128)}) custom-call(bf16[256,256]{1,0:T(8,128)(2,1)} %get-tuple-element.10.proj, bf16[256,256]{1,0:T(8,128)(2,1)} %get-tuple-element.11.dq, bf16[256,256]{1,0:T(8,128)(2,1)} %get-tuple-element.12.dk, ...), custom_call_target="tpu_custom_call" | custom-call | tf_op jit(solution)/shard_map/finish/pallas_call | solution.py:488

commit v3 on v2

--- a/solution.py
+++ b/solution.py
@@ -58,10 +58,10 @@
 def kernel(
     devices, heads, zs, ys,
     q_in, k_in, v_in, go_in, w_in,
-    proj_ref, dq_ref, dk_ref, dv_ref, final,
+    proj_ref, dq_ref, dk_ref, dv_ref, pg_ref,
     q_ref, w_ref, ext, lv1, own, up, gfull,
     edge, e_near, g1, near_out, gu, from_sib, gsum, from_mate, got_near, got2, got3, got4,
-    part, got_part, s_own, s_up, pg32, pg16, got_half, mine, got_z, cross, got_y,
+    part, got_part, s_own, s_up, pg32, pg16, got_half, mine, got_major, lines, final,
     in_sem, row_send, row_recv, grad_send, grad_recv, x_send, x_recv, red_send, red_recv, last_recv,
 ):
     d = lax.axis_index("seq")
@@ -107,11 +107,13 @@
     def y_peer(r):
         return z * (2 * ys) + 2 * lax.rem(y + r, ys) + core
 
-    z_peers = [(z_peer(r), h) for r in range(1, zs)]
-    y_peers = [(y_peer(r), h) for r in range(1, ys)]
+    swap = core == 1
+    major, minor = jnp.where(swap, y, z), jnp.where(swap, z, y)
+    firsts = [(jnp.where(swap, y_peer(r), z_peer(r)), h) for r in range(1, zs)]
+    seconds = [(jnp.where(swap, z_peer(r), y_peer(r)), h) for r in range(1, ys)]
 
     barrier = pltpu.get_barrier_semaphore()
-    everyone = [left, right, mate, *two, *three, *four, *across, *z_peers, *y_peers]
+    everyone = [left, right, mate, *two, *three, *four, *across, *firsts, *seconds]
     for target in everyone:
         pl.semaphore_signal(barrier, inc=1, device_id=target, device_id_type=MESH)
 
@@ -281,8 +283,8 @@
     for i in range(zs):
         window = slice(i * chunk, (i + 1) * chunk)
         mine[i] = (pg32[core, window] + got_half[window].astype(F32)).astype(BF16)
-    for r, target in enumerate(z_peers):
-        send(mine.at[lax.rem(z + r + 1, zs)], got_z.at[r], red_send, red_recv.at[1], target)
+    for r, target in enumerate(firsts):
+        send(mine.at[lax.rem(major + r + 1, zs)], got_major.at[r], red_send, red_recv.at[1], target)
 
     arrived(from_sib, grad_recv.at[5])
     gsum[2 * HALF :] = (gu[pl.ds(pl.multiple_of(mine_part, 16), PART)].astype(F32) + from_sib[HALF:].astype(F32)).astype(BF16)
@@ -326,46 +328,36 @@
     near_out[1, BLOCK:] = g1[2 * HALF : 3 * HALF].astype(BF16)
     send(near_out.at[0], got_near.at[1], grad_send, grad_recv.at[0], left)
     send(near_out.at[1], got_near.at[0], grad_send, grad_recv.at[0], right)
-
+    dq_ref[...] = jnp.concatenate(dq_t, axis=0).T.astype(BF16)
+
+    partial = dot(att16_t.T, w_ref[...])
+    for r in range(heads):
+        part[r] = partial[:, r * FEAT : (r + 1) * FEAT].astype(BF16)
+    for r, target in enumerate(across):
+        send(part.at[target[1]], got_part.at[r], x_send, x_recv.at[1], target)
+
+    arrived(got_major, red_recv.at[1])
+    total = mine[major].astype(F32)
+    for r in range(zs - 1):
+        total = total + got_major[r].astype(F32)
+    lines[minor] = total.astype(BF16)
+    for target in seconds:
+        send(lines.at[minor], lines.at[minor], red_send, red_recv.at[2], target)
     arrived(from_mate, grad_recv.at[6])
     kept = pl.ds(pl.multiple_of(2 * HALF + 96 + (1 - side) * 48, 16), 48)
     gsum[kept] = (gsum[kept].astype(F32) + from_mate[...].astype(F32)).astype(BF16)
     for slot in range(3):
         src = rows_of(gsum, 2 * HALF + 96 + (1 - side) * 48 + slot * 16, 16)
         send(src, got4.at[slot], grad_send, grad_recv.at[4], four[(1, 0, 2)[slot]])
-
-    arrived(got_z, red_recv.at[1])
-    total = mine[z].astype(F32)
-    for r in range(zs - 1):
-        total = total + got_z[r].astype(F32)
-    width = cross.shape[2]
-    for i in range(ys):
-        cross[i] = total[:, i * width : (i + 1) * width].astype(BF16)
-    for r, target in enumerate(y_peers):
-        send(cross.at[lax.rem(y + r + 1, ys)], got_y.at[r], red_send, red_recv.at[2], target)
-
-    partial = dot(att16_t.T, w_ref[...])
-    for r in range(heads):
-        part[r] = partial[:, r * FEAT : (r + 1) * FEAT].astype(BF16)
-    for r, target in enumerate(across):
-        send(part.at[target[1]], got_part.at[r], x_send, x_recv.at[1], target)
-    dq_ref[...] = jnp.concatenate(dq_t, axis=0).T.astype(BF16)
-
-    arrived(got_y, red_recv.at[2])
-    total = cross[y].astype(F32)
-    for r in range(ys - 1):
-        total = total + got_y[r].astype(F32)
-    swap = core == 1
-    first, second = jnp.where(swap, z, y), jnp.where(swap, y, z)
-    block = final.at[core, second, first]
-    final[core, second, first] = total.astype(BF16)
-    for r in range(1, ys):
-        send(block, block, red_send, red_recv.at[3], (jnp.where(swap, z_peer(r), y_peer(r)), h))
-    arrived(got_y, red_recv.at[3])
-    line = final.at[core, second]
-    for r in range(1, zs):
-        send(line, line, red_send, last_recv.at[r - 1], (jnp.where(swap, y_peer(r), z_peer(r)), h))
-    send(line, line, red_send, red_recv.at[4], sibling)
+    arrived(lines.at[: ys - 1], red_recv.at[2])
+    total = lines[0].astype(F32)
+    for i in range(1, ys):
+        total = total + lines[i].astype(F32)
+    line = final.at[core, major]
+    final[core, major] = total.astype(BF16)
+    for r, target in enumerate(firsts):
+        send(line, line, red_send, last_recv.at[r], target)
+    send(line, line, red_send, red_recv.at[3], sibling)
 
     if heads > 1:
         arrived(got_part, x_recv.at[1])
@@ -388,11 +380,14 @@
     dk_ref[...] = rows_grad[:, :FEAT].astype(BF16)
     dv_ref[...] = rows_grad[:, FEAT:].astype(BF16)
 
-    for r in range(1, zs):
+    for r in sorted(range(1, zs), key=lambda r: min(r, zs - r)):
         arrived(line, last_recv.at[r - 1])
-        piece = final.at[core, lax.rem(second + zs - r, zs)]
-        send(piece, piece, red_send, red_recv.at[4], sibling)
-    arrived(final.at[0], red_recv.at[4])
+        piece = final.at[core, lax.rem(major + zs - r, zs)]
+        send(piece, piece, red_send, red_recv.at[3], sibling)
+    arrived(final.at[0], red_recv.at[3])
+    for c in range(2):
+        for i in range(zs):
+            pg_ref[c * BLOCK + i * chunk : c * BLOCK + (i + 1) * chunk] = final[c, i].astype(F32)
 
     arrived(up.at[: 48 + 96 + 2 * HALF], row_send)
     arrived(up.at[: 2 * BLOCK + 2 * HALF], row_send)
@@ -404,28 +399,17 @@
         arrived(gfull.at[0 : heads - 1], x_send)
         arrived(got_part, x_send)
     arrived(got_half, red_send)
-    arrived(got_z, red_send)
-    arrived(got_y, red_send)
-    arrived(got_y, red_send)
+    arrived(got_major, red_send)
+    arrived(lines.at[: ys - 1], red_send)
     arrived(final.at[0, 0 : zs - 1], red_send)
     arrived(final.at[0], red_send)
 
 
-def finish(proj, dq, dk, dv, final, proj_out, dq_out, dk_out, dv_out, pg_out, pg, sems):
-    small = ((proj, proj_out), (dq, dq_out), (dk, dk_out), (dv, dv_out))
-    copies = [pltpu.make_async_copy(src, dst, sems.at[i]) for i, (src, dst) in enumerate(small)]
-    for copy in copies:
+def finish(*refs):
+    results, outs, sems = refs[:5], refs[5:10], refs[10]
+    copies = [pltpu.make_async_copy(src, dst, sems.at[i]) for i, (src, dst) in enumerate(zip(results, outs))]
+    for copy in reversed(copies):
         copy.start()
-    _, zs, ys, chunk, width = final.shape
-    for c in range(2):
-        for zz in range(zs):
-            first = c * BLOCK + zz * chunk
-            for yy in range(ys):
-                piece = final[0, zz, yy] if c == 0 else final[1, yy, zz]
-                pg[first : first + chunk, yy * width : (yy + 1) * width] = piece.astype(F32)
-        half = slice(c * BLOCK, (c + 1) * BLOCK)
-        copies.append(pltpu.make_async_copy(pg.at[half], pg_out.at[half], sems.at[4 + c]))
-        copies[-1].start()
     for copy in copies:
         copy.wait()
 
@@ -434,7 +418,7 @@
     devices = lax.axis_size("seq")
     heads = lax.axis_size("head")
     model = proj_weight.shape[1]
-    chunk, width = BLOCK // zs, model // ys
+    chunk = BLOCK // zs
     vmem = pl.BlockSpec(memory_space=pltpu.VMEM)
     hbm = pl.BlockSpec(memory_space=pltpu.HBM)
     wide = 2 * FEAT
@@ -467,19 +451,19 @@
         ((BLOCK, model), BF16),
         ((zs, chunk, model), BF16),
         ((zs - 1, chunk, model), BF16),
-        ((ys, chunk, width), BF16),
-        ((ys - 1, chunk, width), BF16),
+        ((ys, chunk, model), BF16),
+        ((2, zs, chunk, model), BF16),
     ]
     like = jax.ShapeDtypeStruct
     dma = pltpu.SemaphoreType.DMA
     small = like((ROWS, FEAT), BF16)
     results = pl.pallas_call(
         functools.partial(kernel, devices, heads, zs, ys),
-        out_shape=(small, small, small, small, like((2, zs, ys, chunk, width), BF16)),
+        out_shape=(small, small, small, small, like((FEAT, model), F32)),
         in_specs=[hbm] * 5,
         out_specs=[vmem] * 5,
         scratch_shapes=[pltpu.VMEM(shape, kind) for shape, kind in scratch]
-        + [dma((5,)), dma, dma((7,)), dma, dma((7,)), dma, dma((2,)), dma, dma((5,)), dma((zs - 1,))],
+        + [dma((5,)), dma, dma((7,)), dma, dma((7,)), dma, dma((2,)), dma, dma((4,)), dma((zs - 1,))],
         compiler_params=pltpu.CompilerParams(
             collective_id=0, has_side_effects=True, vmem_limit_bytes=63 * 1024 * 1024
         ),
@@ -490,7 +474,7 @@
         out_shape=(small, small, small, small, like((FEAT, model), F32)),
         in_specs=[vmem] * 5,
         out_specs=[hbm] * 5,
-        scratch_shapes=[pltpu.VMEM((FEAT, model), F32), dma((6,))],
+        scratch_shapes=[dma((5,))],
         name="finish",
     )(*results)
 

time: 66.6 us -> 59.5 us (0.89)
  Pallas kernels: 65.8 us -> 58.7 us
    pallas_call x1, Pallas kernels: 63.3 us -> 56 us  [body(): pl.pallas_call(functools.partial(kernel, devices, heads, zs, ys), out_sha...]
where the time goes in v3:
time: 59.5 us; the launch traced here: 59.4 us
  Pallas kernels  58.7 us (99%)
  between operations  0.64 us (1%)
    pallas_call x1, Pallas kernels, body(): pl.pallas_call(functools.partial(kernel, devices, heads, zs, ys), out_sha...  56 us
    pallas_call x1, Pallas kernels, body(): pl.pallas_call(finish, out_shape=(small, small, small, small, like((FEAT,...  2.68 us

profile of v3, /device:TPU:1, one launch (start us, length us, event | category | flops | bytes accessed | tf_op | source)
XLA Modules:
  0.0 59.4 jit_solution(12249853706422999453)
XLA Ops:
  0.6 56.0 %attention.1 = (bf16[256,256]{1,0:T(8,128)(2,1)}, bf16[256,256]{1,0:T(8,128)(2,1)}, bf16[256,256]{1,0:T(8,128)(2,1)}, bf16[256,256]{1,0:T(8,128)(2,1)}, f32[256,1024]{1,0:T(8,128)}) custom-call(bf16[256,256]{1,0:T(8,128)(2,1)} %q_in.1, bf16[256,256]{1,0:T(8,128)(2,1)} %k_in.1, bf16[256,256]{1,0:T(8,128)(2,1)} %v_in.1, bf16[256,256]{1,0:T(8,128)(2,1)} %go_in.1, ...), custom_call_target="tpu_custom_call" | custom-call | tf_op jit(solution)/shard_map/attention/pallas_call | solution.py:460
  56.7 2.7 %finish.1 = (bf16[256,256]{1,0:T(8,128)(2,1)}, bf16[256,256]{1,0:T(8,128)(2,1)}, bf16[256,256]{1,0:T(8,128)(2,1)}, bf16[256,256]{1,0:T(8,128)(2,1)}, f32[256,1024]{1,0:T(8,128)}) custom-call(bf16[256,256]{1,0:T(8,128)(2,1)} %get-tuple-element.10.refs_0_, bf16[256,256]{1,0:T(8,128)(2,1)} %get-tuple-element.11.refs_1_, ...), custom_call_target="tpu_custom_call" | custom-call | tf_op jit(solution)/shard_map/finish/pallas_call | solution.py:472

commit v4 on v3

--- a/solution.py
+++ b/solution.py
@@ -42,6 +42,17 @@
     row = lax.broadcasted_iota(jnp.int32, (rows // 2, rows), 0)
     column = lax.broadcasted_iota(jnp.int32, (rows // 2, rows), 1)
     return jnp.where((column >= 2 * row) & (column < 2 * row + 2), 0.5, 0.0).astype(BF16)
+
+
+def averages():
+    parts = []
+    for level in range(1, 5):
+        count = ROWS >> level
+        token = lax.broadcasted_iota(jnp.int32, (count, ROWS), 1)
+        first = lax.broadcasted_iota(jnp.int32, (count, ROWS), 0) * (1 << level)
+        inside = (token >= first) & (token < first + (1 << level))
+        parts.append(jnp.where(inside, 0.5**level, 0.0).astype(BF16))
+    return jnp.concatenate(parts, axis=0)
 
 
 def spread_matrix():
@@ -112,11 +123,6 @@
     firsts = [(jnp.where(swap, y_peer(r), z_peer(r)), h) for r in range(1, zs)]
     seconds = [(jnp.where(swap, z_peer(r), y_peer(r)), h) for r in range(1, ys)]
 
-    barrier = pltpu.get_barrier_semaphore()
-    everyone = [left, right, mate, *two, *three, *four, *across, *firsts, *seconds]
-    for target in everyone:
-        pl.semaphore_signal(barrier, inc=1, device_id=target, device_id_type=MESH)
-
     own_rows = ext.at[BLOCK : BLOCK + ROWS]
     loads = [
         (k_in, own_rows.at[:, :FEAT]), (v_in, own_rows.at[:, FEAT:]),
@@ -125,15 +131,16 @@
     loads = [pltpu.make_async_copy(src, dst, in_sem.at[i]) for i, (src, dst) in enumerate(loads)]
     for load in loads:
         load.start()
+
+    barrier = pltpu.get_barrier_semaphore()
+    everyone = [*four, *three, left, right, *two, mate, *across, *firsts, *seconds]
+    for target in everyone:
+        pl.semaphore_signal(barrier, inc=1, device_id=target, device_id_type=MESH)
+
     loads[0].wait()
     loads[1].wait()
 
-    rows = ext[BLOCK : BLOCK + ROWS]
-    offset = 0
-    for level in range(1, 5):
-        rows = dot(pair_average(rows.shape[0]), rows).astype(BF16)
-        own[offset : offset + rows.shape[0]] = rows
-        offset += rows.shape[0]
+    own[...] = dot(averages(), ext[BLOCK : BLOCK + ROWS]).astype(BF16)
     for load in loads[2:]:
         load.wait()
     pl.semaphore_wait(barrier, len(everyone))
@@ -326,8 +333,6 @@
     near_out[0, BLOCK:] = g1[HALF : 2 * HALF].astype(BF16)
     near_out[1, :BLOCK] = (edge[1] + dot(pairs, g1[:HALF].astype(BF16))).astype(BF16)
     near_out[1, BLOCK:] = g1[2 * HALF : 3 * HALF].astype(BF16)
-    send(near_out.at[0], got_near.at[1], grad_send, grad_recv.at[0], left)
-    send(near_out.at[1], got_near.at[0], grad_send, grad_recv.at[0], right)
     dq_ref[...] = jnp.concatenate(dq_t, axis=0).T.astype(BF16)
 
     partial = dot(att16_t.T, w_ref[...])
@@ -343,6 +348,8 @@
     lines[minor] = total.astype(BF16)
     for target in seconds:
         send(lines.at[minor], lines.at[minor], red_send, red_recv.at[2], target)
+    send(near_out.at[0], got_near.at[1], grad_send, grad_recv.at[0], left)
+    send(near_out.at[1], got_near.at[0], grad_send, grad_recv.at[0], right)
     arrived(from_mate, grad_recv.at[6])
     kept = pl.ds(pl.multiple_of(2 * HALF + 96 + (1 - side) * 48, 16), 48)
     gsum[kept] = (gsum[kept].astype(F32) + from_mate[...].astype(F32)).astype(BF16)

time: 59.5 us -> 56.6 us (0.951)
  Pallas kernels: 58.7 us -> 55.7 us
    pallas_call x1, Pallas kernels: 56 us -> 53 us  [body(): pl.pallas_call(functools.partial(kernel, devices, heads, zs, ys), out_sha...]
where the time goes in v4:
time: 56.6 us; the launch traced here: 56.3 us
  Pallas kernels  55.7 us (98%)
  between operations  0.64 us (1%)
    pallas_call x1, Pallas kernels, body(): pl.pallas_call(functools.partial(kernel, devices, heads, zs, ys), out_sha...  53 us
    pallas_call x1, Pallas kernels, body(): pl.pallas_call(finish, out_shape=(small, small, small, small, like((FEAT,...  2.68 us

profile of v4, /device:TPU:1, one launch (start us, length us, event | category | flops | bytes accessed | tf_op | source)
XLA Modules:
  0.0 56.3 jit_solution(15025342418540698625)
XLA Ops:
  0.6 53.0 %attention.1 = (bf16[256,256]{1,0:T(8,128)(2,1)}, bf16[256,256]{1,0:T(8,128)(2,1)}, bf16[256,256]{1,0:T(8,128)(2,1)}, bf16[256,256]{1,0:T(8,128)(2,1)}, f32[256,1024]{1,0:T(8,128)}) custom-call(bf16[256,256]{1,0:T(8,128)(2,1)} %q_in.1, bf16[256,256]{1,0:T(8,128)(2,1)} %k_in.1, bf16[256,256]{1,0:T(8,128)(2,1)} %v_in.1, bf16[256,256]{1,0:T(8,128)(2,1)} %go_in.1, ...), custom_call_target="tpu_custom_call" | custom-call | tf_op jit(solution)/shard_map/attention/pallas_call | solution.py:467
  53.7 2.7 %finish.1 = (bf16[256,256]{1,0:T(8,128)(2,1)}, bf16[256,256]{1,0:T(8,128)(2,1)}, bf16[256,256]{1,0:T(8,128)(2,1)}, bf16[256,256]{1,0:T(8,128)(2,1)}, f32[256,1024]{1,0:T(8,128)}) custom-call(bf16[256,256]{1,0:T(8,128)(2,1)} %get-tuple-element.10.refs_0_, bf16[256,256]{1,0:T(8,128)(2,1)} %get-tuple-element.11.refs_1_, ...), custom_call_target="tpu_custom_call" | custom-call | tf_op jit(solution)/shard_map/finish/pallas_call | solution.py:479

commit v5 on v4

--- a/solution.py
+++ b/solution.py
@@ -69,11 +69,11 @@
 def kernel(
     devices, heads, zs, ys,
     q_in, k_in, v_in, go_in, w_in,
-    proj_ref, dq_ref, dk_ref, dv_ref, pg_ref,
-    q_ref, w_ref, ext, lv1, own, up, gfull,
+    proj_out, dq_out, dk_out, dv_out, pg_out,
+    proj_ref, dq_ref, dk_ref, dv_ref, pg_ref, q_ref, w_ref, ext, lv1, own, up, gfull,
     edge, e_near, g1, near_out, gu, from_sib, gsum, from_mate, got_near, got2, got3, got4,
     part, got_part, s_own, s_up, pg32, pg16, got_half, mine, got_major, lines, final,
-    in_sem, row_send, row_recv, grad_send, grad_recv, x_send, x_recv, red_send, red_recv, last_recv,
+    in_sem, out_sem, row_send, row_recv, grad_send, grad_recv, x_send, x_recv, red_send, red_recv, last_recv, sib_recv,
 ):
     d = lax.axis_index("seq")
     h = lax.axis_index("head")
@@ -96,6 +96,9 @@
 
     def arrived(ref, sem):
         pltpu.make_async_copy(ref, ref, sem).wait()
+
+    def write(src, dst):
+        pltpu.make_async_copy(src, dst, out_sem).start()
 
     def rows_of(ref, first, count):
         return ref.at[pl.ds(pl.multiple_of(first, 16), count)]
@@ -334,6 +337,7 @@
     near_out[1, :BLOCK] = (edge[1] + dot(pairs, g1[:HALF].astype(BF16))).astype(BF16)
     near_out[1, BLOCK:] = g1[2 * HALF : 3 * HALF].astype(BF16)
     dq_ref[...] = jnp.concatenate(dq_t, axis=0).T.astype(BF16)
+    write(dq_ref, dq_out)
 
     partial = dot(att16_t.T, w_ref[...])
     for r in range(heads):
@@ -360,11 +364,18 @@
     total = lines[0].astype(F32)
     for i in range(1, ys):
         total = total + lines[i].astype(F32)
+
+    def store_piece(half, i):
+        window = pl.ds(pl.multiple_of(half * BLOCK + i * chunk, chunk), chunk)
+        pg_ref[window] = final[half, i].astype(F32)
+        write(pg_ref.at[window], pg_out.at[window])
+
     line = final.at[core, major]
     final[core, major] = total.astype(BF16)
     for r, target in enumerate(firsts):
         send(line, line, red_send, last_recv.at[r], target)
-    send(line, line, red_send, red_recv.at[3], sibling)
+    send(line, line, red_send, sib_recv.at[0], sibling)
+    store_piece(core, major)
 
     if heads > 1:
         arrived(got_part, x_recv.at[1])
@@ -372,6 +383,18 @@
     for r in range(heads - 1):
         projected = projected + got_part[r].astype(F32)
     proj_ref[...] = projected.astype(BF16)
+    write(proj_ref, proj_out)
+
+    order = sorted(range(1, zs), key=lambda r: min(r, zs - r))
+
+    def hand_on(distances):
+        for r in distances:
+            arrived(line, last_recv.at[r - 1])
+            piece = final.at[core, lax.rem(major + zs - r, zs)]
+            send(piece, piece, red_send, sib_recv.at[r], sibling)
+            store_piece(core, lax.rem(major + zs - r, zs))
+
+    hand_on(order[:4])
 
     arrived(got4, grad_recv.at[4])
     arrived(got3, grad_recv.at[3])
@@ -386,15 +409,13 @@
         rows_grad = rows_grad + dot(levels[level], total.astype(BF16))
     dk_ref[...] = rows_grad[:, :FEAT].astype(BF16)
     dv_ref[...] = rows_grad[:, FEAT:].astype(BF16)
-
-    for r in sorted(range(1, zs), key=lambda r: min(r, zs - r)):
-        arrived(line, last_recv.at[r - 1])
-        piece = final.at[core, lax.rem(major + zs - r, zs)]
-        send(piece, piece, red_send, red_recv.at[3], sibling)
-    arrived(final.at[0], red_recv.at[3])
-    for c in range(2):
-        for i in range(zs):
-            pg_ref[c * BLOCK + i * chunk : c * BLOCK + (i + 1) * chunk] = final[c, i].astype(F32)
+    write(dk_ref, dk_out)
+    write(dv_ref, dv_out)
+
+    hand_on(order[4:])
+    for r in [0, *order]:
+        arrived(line, sib_recv.at[r])
+        store_piece(1 - core, lax.rem(minor + zs - r, zs))
 
     arrived(up.at[: 48 + 96 + 2 * HALF], row_send)
     arrived(up.at[: 2 * BLOCK + 2 * HALF], row_send)
@@ -410,15 +431,25 @@
     arrived(lines.at[: ys - 1], red_send)
     arrived(final.at[0, 0 : zs - 1], red_send)
     arrived(final.at[0], red_send)
+    for result in (proj_ref, dq_ref, dk_ref, dv_ref, pg_ref):
+        arrived(result, out_sem)
 
 
 def finish(*refs):
-    results, outs, sems = refs[:5], refs[5:10], refs[10]
-    copies = [pltpu.make_async_copy(src, dst, sems.at[i]) for i, (src, dst) in enumerate(zip(results, outs))]
-    for copy in reversed(copies):
-        copy.start()
-    for copy in copies:
-        copy.wait()
+    results, outs, held, load_sems, store_sem = refs[:5], refs[5:10], refs[10:15], refs[15], refs[16]
+    whole = pl.ds(0, ROWS)
+    parts = [(4, pl.ds(i * ROWS // 4, ROWS // 4)) for i in range(4)] + [(i, whole) for i in range(4)]
+    loads = [
+        pltpu.make_async_copy(results[i].at[rows], held[i].at[rows], load_sems.at[n])
+        for n, (i, rows) in enumerate(parts)
+    ]
+    for load in loads:
+        load.start()
+    for load, (i, rows) in zip(loads, parts):
+        load.wait()
+        pltpu.make_async_copy(held[i].at[rows], outs[i].at[rows], store_sem).start()
+    for ref in held:
+        pltpu.make_async_copy(ref, ref, store_sem).wait()
 
 
 def body(zs, ys, queries, keys, values, grad_out, proj_weight):
@@ -426,10 +457,14 @@
     heads = lax.axis_size("head")
     model = proj_weight.shape[1]
     chunk = BLOCK // zs
-    vmem = pl.BlockSpec(memory_space=pltpu.VMEM)
     hbm = pl.BlockSpec(memory_space=pltpu.HBM)
     wide = 2 * FEAT
     scratch = [
+        ((ROWS, FEAT), BF16),
+        ((ROWS, FEAT), BF16),
+        ((ROWS, FEAT), BF16),
+        ((ROWS, FEAT), BF16),
+        ((FEAT, model), F32),
         ((ROWS, FEAT), BF16),
         ((FEAT, model), BF16),
         ((4 * BLOCK, wide), BF16),
@@ -468,9 +503,9 @@
         functools.partial(kernel, devices, heads, zs, ys),
         out_shape=(small, small, small, small, like((FEAT, model), F32)),
         in_specs=[hbm] * 5,
-        out_specs=[vmem] * 5,
+        out_specs=[hbm] * 5,
         scratch_shapes=[pltpu.VMEM(shape, kind) for shape, kind in scratch]
-        + [dma((5,)), dma, dma((7,)), dma, dma((7,)), dma, dma((2,)), dma, dma((4,)), dma((zs - 1,))],
+        + [dma((5,)), dma, dma, dma((7,)), dma, dma((7,)), dma, dma((2,)), dma, dma((3,)), dma((zs - 1,)), dma((zs,))],
         compiler_params=pltpu.CompilerParams(
             collective_id=0, has_side_effects=True, vmem_limit_bytes=63 * 1024 * 1024
         ),
@@ -479,9 +514,9 @@
     return pl.pallas_call(
         finish,
         out_shape=(small, small, small, small, like((FEAT, model), F32)),
-        in_specs=[vmem] * 5,
+        in_specs=[hbm] * 5,
         out_specs=[hbm] * 5,
-        scratch_shapes=[dma((5,))],
+        scratch_shapes=[pltpu.VMEM((ROWS, FEAT), BF16)] * 4 + [pltpu.VMEM((FEAT, model), F32), dma((8,)), dma],
         name="finish",
     )(*results)
 

time: 56.6 us -> 55.8 us (0.986)
  Pallas kernels: 55.7 us -> 55 us
where the time goes in v5:
time: 55.8 us; the launch traced here: 55.7 us
  Pallas kernels  55 us (99%)
  between operations  0.64 us (1%)
    pallas_call x1, Pallas kernels, body(): pl.pallas_call(functools.partial(kernel, devices, heads, zs, ys), out_sha...  52.9 us
    pallas_call x1, Pallas kernels, body(): pl.pallas_call(finish, out_shape=(small, small, small, small, like((FEAT,...  2.16 us

profile of v5, /device:TPU:1, one launch (start us, length us, event | category | flops | bytes accessed | tf_op | source)
XLA Modules:
  0.0 55.7 jit_solution(6697959236727071055)
XLA Ops:
  0.6 52.9 %attention.1 = (bf16[256,256]{1,0:T(8,128)(2,1)}, bf16[256,256]{1,0:T(8,128)(2,1)}, bf16[256,256]{1,0:T(8,128)(2,1)}, bf16[256,256]{1,0:T(8,128)(2,1)}, f32[256,1024]{1,0:T(8,128)}) custom-call(bf16[256,256]{1,0:T(8,128)(2,1)} %q_in.1, bf16[256,256]{1,0:T(8,128)(2,1)} %k_in.1, bf16[256,256]{1,0:T(8,128)(2,1)} %v_in.1, bf16[256,256]{1,0:T(8,128)(2,1)} %go_in.1, ...), custom_call_target="tpu_custom_call" | custom-call | tf_op jit(solution)/shard_map/attention/pallas_call | solution.py:502
  53.5 2.2 %finish.1 = (bf16[256,256]{1,0:T(8,128)(2,1)}, bf16[256,256]{1,0:T(8,128)(2,1)}, bf16[256,256]{1,0:T(8,128)(2,1)}, bf16[256,256]{1,0:T(8,128)(2,1)}, f32[256,1024]{1,0:T(8,128)}) custom-call(bf16[256,256]{1,0:T(8,128)(2,1)} %get-tuple-element.10.refs_0_, bf16[256,256]{1,0:T(8,128)(2,1)} %get-tuple-element.11.refs_1_, ...), custom_call_target="tpu_custom_call" | custom-call | tf_op jit(solution)/shard_map/finish/pallas_call | solution.py:514

commit v6 on v5

--- a/solution.py
+++ b/solution.py
@@ -289,12 +289,15 @@
     send(gu.at[2 * HALF : 3 * HALF], from_sib.at[:HALF], grad_send, grad_recv.at[5], sibling)
 
     arrived(got_half, red_recv.at[0])
-    chunk = BLOCK // zs
-    for i in range(zs):
-        window = slice(i * chunk, (i + 1) * chunk)
-        mine[i] = (pg32[core, window] + got_half[window].astype(F32)).astype(BF16)
-    for r, target in enumerate(firsts):
-        send(mine.at[lax.rem(major + r + 1, zs)], got_major.at[r], red_send, red_recv.at[1], target)
+    chunk, width = BLOCK // zs, mine.shape[3]
+    for p in range(2):
+        cols = slice(p * width, (p + 1) * width)
+        for i in range(zs):
+            window = slice(i * chunk, (i + 1) * chunk)
+            mine[p, i] = (pg32[core, window, cols] + got_half[window, cols].astype(F32)).astype(BF16)
+        for r, target in enumerate(firsts):
+            src = mine.at[p, lax.rem(major + r + 1, zs)]
+            send(src, got_major.at[p, r], red_send, red_recv.at[1 + p], target)
 
     arrived(from_sib, grad_recv.at[5])
     gsum[2 * HALF :] = (gu[pl.ds(pl.multiple_of(mine_part, 16), PART)].astype(F32) + from_sib[HALF:].astype(F32)).astype(BF16)
@@ -345,13 +348,14 @@
     for r, target in enumerate(across):
         send(part.at[target[1]], got_part.at[r], x_send, x_recv.at[1], target)
 
-    arrived(got_major, red_recv.at[1])
-    total = mine[major].astype(F32)
-    for r in range(zs - 1):
-        total = total + got_major[r].astype(F32)
-    lines[minor] = total.astype(BF16)
-    for target in seconds:
-        send(lines.at[minor], lines.at[minor], red_send, red_recv.at[2], target)
+    for p in range(2):
+        arrived(got_major.at[p], red_recv.at[1 + p])
+        total = mine[p, major].astype(F32)
+        for r in range(zs - 1):
+            total = total + got_major[p, r].astype(F32)
+        lines[p, minor] = total.astype(BF16)
+        for target in seconds:
+            send(lines.at[p, minor], lines.at[p, minor], red_send, red_recv.at[3 + p], target)
     send(near_out.at[0], got_near.at[1], grad_send, grad_recv.at[0], left)
     send(near_out.at[1], got_near.at[0], grad_send, grad_recv.at[0], right)
     arrived(from_mate, grad_recv.at[6])
@@ -360,22 +364,25 @@
     for slot in range(3):
         src = rows_of(gsum, 2 * HALF + 96 + (1 - side) * 48 + slot * 16, 16)
         send(src, got4.at[slot], grad_send, grad_recv.at[4], four[(1, 0, 2)[slot]])
-    arrived(lines.at[: ys - 1], red_recv.at[2])
-    total = lines[0].astype(F32)
-    for i in range(1, ys):
-        total = total + lines[i].astype(F32)
-
-    def store_piece(half, i):
-        window = pl.ds(pl.multiple_of(half * BLOCK + i * chunk, chunk), chunk)
-        pg_ref[window] = final[half, i].astype(F32)
-        write(pg_ref.at[window], pg_out.at[window])
-
-    line = final.at[core, major]
-    final[core, major] = total.astype(BF16)
-    for r, target in enumerate(firsts):
-        send(line, line, red_send, last_recv.at[r], target)
-    send(line, line, red_send, sib_recv.at[0], sibling)
-    store_piece(core, major)
+
+    def store_piece(half, p, i):
+        rows = pl.ds(pl.multiple_of(half * BLOCK + i * chunk, chunk), chunk)
+        cols = slice(p * width, (p + 1) * width)
+        pg_ref[rows, cols] = final[half, p, i].astype(F32)
+        write(pg_ref.at[rows, cols], pg_out.at[rows, cols])
+
+    line = final.at[core, 0, major]
+    for p in range(2):
+        arrived(lines.at[p, : ys - 1], red_recv.at[3 + p])
+        total = lines[p, 0].astype(F32)
+        for i in range(1, ys):
+            total = total + lines[p, i].astype(F32)
+        piece = final.at[core, p, major]
+        final[core, p, major] = total.astype(BF16)
+        for r, target in enumerate(firsts):
+            send(piece, piece, red_send, last_recv.at[p, r], target)
+        send(piece, piece, red_send, sib_recv.at[p, 0], sibling)
+        store_piece(core, p, major)
 
     if heads > 1:
         arrived(got_part, x_recv.at[1])
@@ -389,10 +396,12 @@
 
     def hand_on(distances):
         for r in distances:
-            arrived(line, last_recv.at[r - 1])
-            piece = final.at[core, lax.rem(major + zs - r, zs)]
-            send(piece, piece, red_send, sib_recv.at[r], sibling)
-            store_piece(core, lax.rem(major + zs - r, zs))
+            for p in range(2):
+                arrived(line, last_recv.at[p, r - 1])
+                i = lax.rem(major + zs - r, zs)
+                piece = final.at[core, p, i]
+                send(piece, piece, red_send, sib_recv.at[p, r], sibling)
+                store_piece(core, p, i)
 
     hand_on(order[:4])
 
@@ -414,8 +423,9 @@
 
     hand_on(order[4:])
     for r in [0, *order]:
-        arrived(line, sib_recv.at[r])
-        store_piece(1 - core, lax.rem(minor + zs - r, zs))
+        for p in range(2):
+            arrived(line, sib_recv.at[p, r])
+            store_piece(1 - core, p, lax.rem(minor + zs - r, zs))
 
     arrived(up.at[: 48 + 96 + 2 * HALF], row_send)
     arrived(up.at[: 2 * BLOCK + 2 * HALF], row_send)
@@ -428,8 +438,8 @@
         arrived(got_part, x_send)
     arrived(got_half, red_send)
     arrived(got_major, red_send)
-    arrived(lines.at[: ys - 1], red_send)
-    arrived(final.at[0, 0 : zs - 1], red_send)
+    arrived(lines.at[:, : ys - 1], red_send)
+    arrived(final.at[0, :, : zs - 1], red_send)
     arrived(final.at[0], red_send)
     for result in (proj_ref, dq_ref, dk_ref, dv_ref, pg_ref):
         arrived(result, out_sem)
@@ -491,10 +501,10 @@
         ((2, BLOCK, model), F32),
         ((2, BLOCK, model), BF16),
         ((BLOCK, model), BF16),
-        ((zs, chunk, model), BF16),
-        ((zs - 1, chunk, model), BF16),
-        ((ys, chunk, model), BF16),
-        ((2, zs, chunk, model), BF16),
+        ((2, zs, chunk, model // 2), BF16),
+        ((2, zs - 1, chunk, model // 2), BF16),
+        ((2, ys, chunk, model // 2), BF16),
+        ((2, 2, zs, chunk, model // 2), BF16),
     ]
     like = jax.ShapeDtypeStruct
     dma = pltpu.SemaphoreType.DMA
@@ -505,7 +515,7 @@
         in_specs=[hbm] * 5,
         out_specs=[hbm] * 5,
         scratch_shapes=[pltpu.VMEM(shape, kind) for shape, kind in scratch]
-        + [dma((5,)), dma, dma, dma((7,)), dma, dma((7,)), dma, dma((2,)), dma, dma((3,)), dma((zs - 1,)), dma((zs,))],
+        + [dma((5,)), dma, dma, dma((7,)), dma, dma((7,)), dma, dma((2,)), dma, dma((5,)), dma((2, zs - 1)), dma((2, zs))],
         compiler_params=pltpu.CompilerParams(
             collective_id=0, has_side_effects=True, vmem_limit_bytes=63 * 1024 * 1024
         ),

time: 55.8 us -> 54.9 us (0.984)
  Pallas kernels: 55 us -> 53.7 us
    pallas_call x1, Pallas kernels: 52.9 us -> 51.5 us  [body(): pl.pallas_call(functools.partial(kernel, devices, heads, zs, ys), out_sha...]
where the time goes in v6:
time: 54.9 us; the launch traced here: 54.3 us
  Pallas kernels  53.7 us (98%)
  between operations  0.64 us (1%)
    pallas_call x1, Pallas kernels, body(): pl.pallas_call(functools.partial(kernel, devices, heads, zs, ys), out_sha...  51.5 us
    pallas_call x1, Pallas kernels, body(): pl.pallas_call(finish, out_shape=(small, small, small, small, like((FEAT,...  2.16 us

profile of v6, /device:TPU:1, one launch (start us, length us, event | category | flops | bytes accessed | tf_op | source)
XLA Modules:
  0.0 54.3 jit_solution(9821372897208933658)
XLA Ops:
  0.6 51.5 %attention.1 = (bf16[256,256]{1,0:T(8,128)(2,1)}, bf16[256,256]{1,0:T(8,128)(2,1)}, bf16[256,256]{1,0:T(8,128)(2,1)}, bf16[256,256]{1,0:T(8,128)(2,1)}, f32[256,1024]{1,0:T(8,128)}) custom-call(bf16[256,256]{1,0:T(8,128)(2,1)} %q_in.1, bf16[256,256]{1,0:T(8,128)(2,1)} %k_in.1, bf16[256,256]{1,0:T(8,128)(2,1)} %v_in.1, bf16[256,256]{1,0:T(8,128)(2,1)} %go_in.1, ...), custom_call_target="tpu_custom_call" | custom-call | tf_op jit(solution)/shard_map/attention/pallas_call | solution.py:512
  52.2 2.2 %finish.1 = (bf16[256,256]{1,0:T(8,128)(2,1)}, bf16[256,256]{1,0:T(8,128)(2,1)}, bf16[256,256]{1,0:T(8,128)(2,1)}, bf16[256,256]{1,0:T(8,128)(2,1)}, f32[256,1024]{1,0:T(8,128)}) custom-call(bf16[256,256]{1,0:T(8,128)(2,1)} %get-tuple-element.10.refs_0_, bf16[256,256]{1,0:T(8,128)(2,1)} %get-tuple-element.11.refs_1_, ...), custom_call_target="tpu_custom_call" | custom-call | tf_op jit(solution)/shard_map/finish/pallas_call | solution.py:524

commit v7 on v6

--- a/solution.py
+++ b/solution.py
@@ -125,6 +125,7 @@
     major, minor = jnp.where(swap, y, z), jnp.where(swap, z, y)
     firsts = [(jnp.where(swap, y_peer(r), z_peer(r)), h) for r in range(1, zs)]
     seconds = [(jnp.where(swap, z_peer(r), y_peer(r)), h) for r in range(1, ys)]
+    far_first = sorted(range(1, zs), key=lambda r: -min(r, zs - r))
 
     own_rows = ext.at[BLOCK : BLOCK + ROWS]
     loads = [
@@ -136,7 +137,8 @@
         load.start()
 
     barrier = pltpu.get_barrier_semaphore()
-    everyone = [*four, *three, left, right, *two, mate, *across, *firsts, *seconds]
+    rings = [peer for r in far_first for peer in (firsts[r - 1], seconds[r - 1])]
+    everyone = [*rings[:2], *four, *three, *rings[2:6], *two, left, right, mate, *across, *rings[6:]]
     for target in everyone:
         pl.semaphore_signal(barrier, inc=1, device_id=target, device_id_type=MESH)
 
@@ -152,7 +154,7 @@
     for slot in range(3):
         dst = rows_of(up, mine_part + 96 + side * 48 + slot * 16, 16)
         send(own.at[224:240], dst, row_send, row_recv.at[4], four[slot])
-    for slot in range(3):
+    for slot in (2, 0, 1):
         dst = rows_of(up, mine_part + slot * 32, 32)
         send(own.at[192:224], dst, row_send, row_recv.at[3], three[slot])
     for slot in range(2):
@@ -295,9 +297,9 @@
         for i in range(zs):
             window = slice(i * chunk, (i + 1) * chunk)
             mine[p, i] = (pg32[core, window, cols] + got_half[window, cols].astype(F32)).astype(BF16)
-        for r, target in enumerate(firsts):
-            src = mine.at[p, lax.rem(major + r + 1, zs)]
-            send(src, got_major.at[p, r], red_send, red_recv.at[1 + p], target)
+        for r in far_first:
+            src = mine.at[p, lax.rem(major + r, zs)]
+            send(src, got_major.at[p, r - 1], red_send, red_recv.at[1 + p], firsts[r - 1])
 
     arrived(from_sib, grad_recv.at[5])
     gsum[2 * HALF :] = (gu[pl.ds(pl.multiple_of(mine_part, 16), PART)].astype(F32) + from_sib[HALF:].astype(F32)).astype(BF16)
@@ -354,8 +356,8 @@
         for r in range(zs - 1):
             total = total + got_major[p, r].astype(F32)
         lines[p, minor] = total.astype(BF16)
-        for target in seconds:
-            send(lines.at[p, minor], lines.at[p, minor], red_send, red_recv.at[3 + p], target)
+        for r in far_first:
+            send(lines.at[p, minor], lines.at[p, minor], red_send, red_recv.at[3 + p], seconds[r - 1])
     send(near_out.at[0], got_near.at[1], grad_send, grad_recv.at[0], left)
     send(near_out.at[1], got_near.at[0], grad_send, grad_recv.at[0], right)
     arrived(from_mate, grad_recv.at[6])
@@ -379,8 +381,8 @@
             total = total + lines[p, i].astype(F32)
         piece = final.at[core, p, major]
         final[core, p, major] = total.astype(BF16)
-        for r, target in enumerate(firsts):
-            send(piece, piece, red_send, last_recv.at[p, r], target)
+        for r in far_first:
+            send(piece, piece, red_send, last_recv.at[p, r - 1], firsts[r - 1])
         send(piece, piece, red_send, sib_recv.at[p, 0], sibling)
         store_piece(core, p, major)
 

time: 54.9 us -> 54.5 us (level)
  no operation moved by 1% of the time
where the time goes in v7:
time: 54.5 us; the launch traced here: 53.8 us
  Pallas kernels  53.2 us (98%)
  between operations  0.64 us (1%)
    pallas_call x1, Pallas kernels, body(): pl.pallas_call(functools.partial(kernel, devices, heads, zs, ys), out_sha...  51 us
    pallas_call x1, Pallas kernels, body(): pl.pallas_call(finish, out_shape=(small, small, small, small, like((FEAT,...  2.16 us

profile of v7, /device:TPU:1, one launch (start us, length us, event | category | flops | bytes accessed | tf_op | source)
XLA Modules:
  0.0 53.8 jit_solution(7564147686357169367)
XLA Ops:
  0.6 51.0 %attention.1 = (bf16[256,256]{1,0:T(8,128)(2,1)}, bf16[256,256]{1,0:T(8,128)(2,1)}, bf16[256,256]{1,0:T(8,128)(2,1)}, bf16[256,256]{1,0:T(8,128)(2,1)}, f32[256,1024]{1,0:T(8,128)}) custom-call(bf16[256,256]{1,0:T(8,128)(2,1)} %q_in.1, bf16[256,256]{1,0:T(8,128)(2,1)} %k_in.1, bf16[256,256]{1,0:T(8,128)(2,1)} %v_in.1, bf16[256,256]{1,0:T(8,128)(2,1)} %go_in.1, ...), custom_call_target="tpu_custom_call" | custom-call | tf_op jit(solution)/shard_map/attention/pallas_call | solution.py:514
  51.7 2.2 %finish.1 = (bf16[256,256]{1,0:T(8,128)(2,1)}, bf16[256,256]{1,0:T(8,128)(2,1)}, bf16[256,256]{1,0:T(8,128)(2,1)}, bf16[256,256]{1,0:T(8,128)(2,1)}, f32[256,1024]{1,0:T(8,128)}) custom-call(bf16[256,256]{1,0:T(8,128)(2,1)} %get-tuple-element.10.refs_0_, bf16[256,256]{1,0:T(8,128)(2,1)} %get-tuple-element.11.refs_1_, ...), custom_call_target="tpu_custom_call" | custom-call | tf_op jit(solution)/shard_map/finish/pallas_call | solution.py:526

commit v8 on v7

--- a/solution.py
+++ b/solution.py
@@ -18,6 +18,7 @@
 OWN_KEYS = NEAR + 3 * HALF
 UPPER = 9 * HALF
 PART = 3 * 32 + 6 * 16
+PIECES = 4
 NEG = -1e30
 SCALE = 1.0 / math.sqrt(HEAD_DIM)
 EXP2_SCALE = SCALE * math.log2(math.e)
@@ -292,7 +293,7 @@
 
     arrived(got_half, red_recv.at[0])
     chunk, width = BLOCK // zs, mine.shape[3]
-    for p in range(2):
+    for p in range(PIECES):
         cols = slice(p * width, (p + 1) * width)
         for i in range(zs):
             window = slice(i * chunk, (i + 1) * chunk)
@@ -350,14 +351,14 @@
     for r, target in enumerate(across):
         send(part.at[target[1]], got_part.at[r], x_send, x_recv.at[1], target)
 
-    for p in range(2):
+    for p in range(PIECES):
         arrived(got_major.at[p], red_recv.at[1 + p])
         total = mine[p, major].astype(F32)
         for r in range(zs - 1):
             total = total + got_major[p, r].astype(F32)
         lines[p, minor] = total.astype(BF16)
         for r in far_first:
-            send(lines.at[p, minor], lines.at[p, minor], red_send, red_recv.at[3 + p], seconds[r - 1])
+            send(lines.at[p, minor], lines.at[p, minor], red_send, red_recv.at[1 + PIECES + p], seconds[r - 1])
     send(near_out.at[0], got_near.at[1], grad_send, grad_recv.at[0], left)
     send(near_out.at[1], got_near.at[0], grad_send, grad_recv.at[0], right)
     arrived(from_mate, grad_recv.at[6])
@@ -374,8 +375,8 @@
         write(pg_ref.at[rows, cols], pg_out.at[rows, cols])
 
     line = final.at[core, 0, major]
-    for p in range(2):
-        arrived(lines.at[p, : ys - 1], red_recv.at[3 + p])
+    for p in range(PIECES):
+        arrived(lines.at[p, : ys - 1], red_recv.at[1 + PIECES + p])
         total = lines[p, 0].astype(F32)
         for i in range(1, ys):
             total = total + lines[p, i].astype(F32)
@@ -398,7 +399,7 @@
 
     def hand_on(distances):
         for r in distances:
-            for p in range(2):
+            for p in range(PIECES):
                 arrived(line, last_recv.at[p, r - 1])
                 i = lax.rem(major + zs - r, zs)
                 piece = final.at[core, p, i]
@@ -425,7 +426,7 @@
 
     hand_on(order[4:])
     for r in [0, *order]:
-        for p in range(2):
+        for p in range(PIECES):
             arrived(line, sib_recv.at[p, r])
             store_piece(1 - core, p, lax.rem(minor + zs - r, zs))
 
@@ -503,10 +504,10 @@
         ((2, BLOCK, model), F32),
         ((2, BLOCK, model), BF16),
         ((BLOCK, model), BF16),
-        ((2, zs, chunk, model // 2), BF16),
-        ((2, zs - 1, chunk, model // 2), BF16),
-        ((2, ys, chunk, model // 2), BF16),
-        ((2, 2, zs, chunk, model // 2), BF16),
+        ((PIECES, zs, chunk, model // PIECES), BF16),
+        ((PIECES, zs - 1, chunk, model // PIECES), BF16),
+        ((PIECES, ys, chunk, model // PIECES), BF16),
+        ((2, PIECES, zs, chunk, model // PIECES), BF16),
     ]
     like = jax.ShapeDtypeStruct
     dma = pltpu.SemaphoreType.DMA
@@ -517,7 +518,7 @@
         in_specs=[hbm] * 5,
         out_specs=[hbm] * 5,
         scratch_shapes=[pltpu.VMEM(shape, kind) for shape, kind in scratch]
-        + [dma((5,)), dma, dma, dma((7,)), dma, dma((7,)), dma, dma((2,)), dma, dma((5,)), dma((2, zs - 1)), dma((2, zs))],
+        + [dma((5,)), dma, dma, dma((7,)), dma, dma((7,)), dma, dma((2,)), dma, dma((1 + 2 * PIECES,)), dma((PIECES, zs - 1)), dma((PIECES, zs))],
         compiler_params=pltpu.CompilerParams(
             collective_id=0, has_side_effects=True, vmem_limit_bytes=63 * 1024 * 1024
         ),

time: 54.5 us -> 54.8 us (level)
  no operation moved by 1% of the time
where the time goes in v8:
time: 54.8 us; the launch traced here: 53.8 us
  Pallas kernels  53.2 us (97%)
  between operations  0.64 us (1%)
    pallas_call x1, Pallas kernels, body(): pl.pallas_call(functools.partial(kernel, devices, heads, zs, ys), out_sha...  51 us
    pallas_call x1, Pallas kernels, body(): pl.pallas_call(finish, out_shape=(small, small, small, small, like((FEAT,...  2.16 us

profile of v8, /device:TPU:1, one launch (start us, length us, event | category | flops | bytes accessed | tf_op | source)
XLA Modules:
  0.0 53.8 jit_solution(14609150787829847138)
XLA Ops:
  0.6 51.0 %attention.1 = (bf16[256,256]{1,0:T(8,128)(2,1)}, bf16[256,256]{1,0:T(8,128)(2,1)}, bf16[256,256]{1,0:T(8,128)(2,1)}, bf16[256,256]{1,0:T(8,128)(2,1)}, f32[256,1024]{1,0:T(8,128)}) custom-call(bf16[256,256]{1,0:T(8,128)(2,1)} %q_in.1, bf16[256,256]{1,0:T(8,128)(2,1)} %k_in.1, bf16[256,256]{1,0:T(8,128)(2,1)} %v_in.1, bf16[256,256]{1,0:T(8,128)(2,1)} %go_in.1, ...), custom_call_target="tpu_custom_call" | custom-call | tf_op jit(solution)/shard_map/attention/pallas_call | solution.py:515
  51.7 2.2 %finish.1 = (bf16[256,256]{1,0:T(8,128)(2,1)}, bf16[256,256]{1,0:T(8,128)(2,1)}, bf16[256,256]{1,0:T(8,128)(2,1)}, bf16[256,256]{1,0:T(8,128)(2,1)}, f32[256,1024]{1,0:T(8,128)}) custom-call(bf16[256,256]{1,0:T(8,128)(2,1)} %get-tuple-element.10.refs_0_, bf16[256,256]{1,0:T(8,128)(2,1)} %get-tuple-element.11.refs_1_, ...), custom_call_target="tpu_custom_call" | custom-call | tf_op jit(solution)/shard_map/finish/pallas_call | solution.py:527
